TPU v7x, 128 devices: a whole 4x4x4 slice. The times are simulated.
128 devices in a mesh: ctx: 16 (over y, x_hi, core), fsdp: 8 (over z, x_lo).
Axes of the slice: x: 4 (x_hi: 2, x_lo: 2; x = x_hi * 2 + x_lo), y: 4, z: 4, core: 2. Of those that a mesh axis runs over, the one named last changes fastest.
Arguments:
- inputs: bfloat16 [8, 2048, 1024], P('fsdp', 'ctx'), may hold values from -4 to 4, as said below
- w_query: bfloat16 [1024, 1024], P('fsdp'), may hold values from -0.176776695 to 0.176776695
- b_query: bfloat16 [1024], P('fsdp'), may hold values from -4 to 4
- w_key: bfloat16 [1024, 1024], P('fsdp'), may hold values from -0.176776695 to 0.176776695
- w_value: bfloat16 [1024, 1024], P('fsdp'), may hold values from -0.1875 to 0.1875
- b_value: bfloat16 [1024], P('fsdp'), may hold values from -4 to 4
- w_out: bfloat16 [1024, 1024], P('fsdp'), may hold values from -6 to 6
- b_out: bfloat16 [1024], P('fsdp'), may hold values from -4 to 4
- gain_one: bfloat16 [1024], P('fsdp'), may hold values from 0.5 to 1.5
- shift_one: bfloat16 [1024], P('fsdp'), may hold values from -4 to 4
- w_up: bfloat16 [1024, 4096], P('fsdp'), may hold values from -0.1875 to 0.1875
- b_up: bfloat16 [4096], P('fsdp'), may hold values from -4 to 4
- w_down: bfloat16 [4096, 1024], P('fsdp'), may hold values from -0.125 to 0.125
- b_down: bfloat16 [1024], P('fsdp'), may hold values from -4 to 4
- gain_two: bfloat16 [1024], P('fsdp'), may hold values from 0.5 to 1.5
- shift_two: bfloat16 [1024], P('fsdp'), may hold values from -4 to 4
- cotangent: bfloat16 [8, 2048, 1024], P('fsdp', 'ctx'), may hold values from -6 to 6
Outputs:
- output: bfloat16 [8, 2048, 1024], P('fsdp', 'ctx')
- grad_inputs: float32 [8, 2048, 1024], P('fsdp', 'ctx')
- grad_w_query: float32 [1024, 1024], P('fsdp')
- grad_b_query: float32 [1024], P('fsdp')
- grad_w_key: float32 [1024, 1024], P('fsdp')
- grad_w_value: float32 [1024, 1024], P('fsdp')
- grad_b_value: float32 [1024], P('fsdp')
- grad_w_out: float32 [1024, 1024], P('fsdp')
- grad_b_out: float32 [1024], P('fsdp')
- grad_gain_one: float32 [1024], P('fsdp')
- grad_shift_one: float32 [1024], P('fsdp')
- grad_w_up: float32 [1024, 4096], P('fsdp')
- grad_b_up: float32 [4096], P('fsdp')
- grad_w_down: float32 [4096, 1024], P('fsdp')
- grad_b_down: float32 [1024], P('fsdp')
- grad_gain_two: float32 [1024], P('fsdp')
- grad_shift_two: float32 [1024], P('fsdp')
Inputs may be any that keep to these rules, and one draw needn't show every extreme that they name: `inputs`: independent entries of mean 0 and deviation 1.
All inputs are finite; a program needn't handle non-finite values.
Results may differ from a plain program's by a relative error of at most 0.024.
Values may be sent and summed in bfloat16 or wider, within the bound.
No kernel may reach another device: no remote copies, remote signals or barrier semaphores. Data moves between devices by JAX's collectives and lax.ppermute only.
A program may use at most 192 MiB of HBM per device.

v0:
```python
import jax
import jax.numpy as jnp
from jax import lax
from jax.sharding import PartitionSpec as P

HEADS = 16


EPSILON = 1e-05


def shifted(block, axis, distance):
    devices = range(lax.axis_size(axis))
    route = [((i - distance) % len(devices), i) for i in devices]
    return lax.ppermute(block, axis, route)


def norm_rows(hidden, gain, shift):
    center = hidden - jnp.mean(hidden, axis=-1, keepdims=True)
    spread = jnp.mean(center * center, axis=-1, keepdims=True)
    return center * lax.rsqrt(spread + EPSILON) * gain + shift


def multiply(matrix, other):
    return jnp.dot(matrix, other, preferred_element_type=jnp.float32)


def inner_rows(matrix, other):
    return lax.dot_general(
        matrix, other, (((0,), (0,)), ((), ())), preferred_element_type=jnp.float32
    )


def times_back(matrix, other):
    return lax.dot_general(
        matrix, other, (((1,), (1,)), ((), ())), preferred_element_type=jnp.float32
    )


def column_sum(grad):
    return jnp.sum(grad.astype(jnp.float32), axis=0)


def on_device(
    inputs,
    w_query,
    b_query,
    w_key,
    w_value,
    b_value,
    w_out,
    b_out,
    gain_one,
    shift_one,
    w_up,
    b_up,
    w_down,
    b_down,
    gain_two,
    shift_two,
    cotangent,
):
    low_type = jnp.bfloat16
    gathered = (
        lax.all_gather(w_query, "fsdp", axis=0, tiled=True),
        lax.all_gather(b_query, "fsdp", axis=0, tiled=True),
        lax.all_gather(w_key, "fsdp", axis=0, tiled=True),
        lax.all_gather(w_value, "fsdp", axis=0, tiled=True),
        lax.all_gather(b_value, "fsdp", axis=0, tiled=True),
        lax.all_gather(w_out, "fsdp", axis=0, tiled=True),
        lax.all_gather(b_out, "fsdp", axis=0, tiled=True),
        lax.all_gather(gain_one, "fsdp", axis=0, tiled=True),
        lax.all_gather(shift_one, "fsdp", axis=0, tiled=True),
        lax.all_gather(w_up, "fsdp", axis=0, tiled=True),
        lax.all_gather(b_up, "fsdp", axis=0, tiled=True),
        lax.all_gather(w_down, "fsdp", axis=0, tiled=True),
        lax.all_gather(b_down, "fsdp", axis=0, tiled=True),
        lax.all_gather(gain_two, "fsdp", axis=0, tiled=True),
        lax.all_gather(shift_two, "fsdp", axis=0, tiled=True),
    )
    (
        mat_query,
        vec_query,
        mat_key,
        mat_value,
        vec_value,
        mat_out,
        vec_out,
        gain_a,
        shift_a,
        mat_up,
        vec_up,
        mat_down,
        vec_down,
        gain_b,
        shift_b,
    ) = gathered
    seq_count, tok_count, model_width = inputs.shape
    head_count = HEADS
    head_size = model_width // head_count
    scaling = head_size ** (-0.5)
    row_count = seq_count * tok_count
    tok_rows = inputs.reshape(row_count, model_width)
    query_rows = ((multiply(tok_rows, mat_query) + vec_query) * scaling).astype(low_type)
    key_rows = multiply(tok_rows, mat_key).astype(low_type)
    value_rows = (multiply(tok_rows, mat_value) + vec_value).astype(low_type)
    query_heads = query_rows.reshape(seq_count, tok_count, head_count, head_size)
    start_top = jnp.full((seq_count, head_count, tok_count), -1e30, jnp.float32)
    key_block = key_rows.reshape(seq_count, tok_count, model_width)
    value_block = value_rows.reshape(seq_count, tok_count, model_width)
    run_top = start_top
    key_part = lax.all_gather(key_block, "ctx", axis=1, tiled=True).reshape(
        seq_count, -1, head_count, head_size
    )
    value_part = lax.all_gather(value_block, "ctx", axis=1, tiled=True).reshape(
        seq_count, -1, head_count, head_size
    )
    scores = jnp.einsum(
        "sqhe,skhe->shqk", query_heads, key_part, preferred_element_type=jnp.float32
    )
    new_peak = jnp.maximum(run_top, jnp.max(scores, axis=-1))
    weights = jnp.exp(scores - new_peak[..., None])
    run_total = jnp.sum(weights, axis=-1)
    run_acc = jnp.einsum(
        "shqk,skhe->shqe", weights.astype(low_type), value_part, preferred_element_type=jnp.float32
    )
    run_top, run_total, run_acc = (new_peak, run_total, run_acc)
    log_total = run_top + jnp.log(run_total)
    context_heads = jnp.transpose(run_acc / run_total[..., None], (0, 2, 1, 3))
    context_low = context_heads.reshape(row_count, model_width).astype(low_type)
    branch = multiply(context_low, mat_out) + vec_out
    pre_one = tok_rows.astype(jnp.float32) + branch
    first, back_one = jax.vjp(
        norm_rows, pre_one, gain_a.astype(jnp.float32), shift_a.astype(jnp.float32)
    )
    first_low = first.astype(low_type)
    hidden = multiply(first_low, mat_up) + vec_up
    active_f, back_gelu = jax.vjp(lambda value: jax.nn.gelu(value, approximate=False), hidden)
    active = active_f.astype(low_type)
    second = multiply(active, mat_down) + vec_down
    pre_two = first + second
    result, back_two = jax.vjp(
        norm_rows, pre_two, gain_b.astype(jnp.float32), shift_b.astype(jnp.float32)
    )
    again = (
        lax.all_gather(w_out, "fsdp", axis=0, tiled=True),
        lax.all_gather(w_up, "fsdp", axis=0, tiled=True),
        lax.all_gather(w_down, "fsdp", axis=0, tiled=True),
        lax.all_gather(w_query, "fsdp", axis=0, tiled=True),
        lax.all_gather(w_key, "fsdp", axis=0, tiled=True),
        lax.all_gather(w_value, "fsdp", axis=0, tiled=True),
    )
    mat_out, mat_up, mat_down, mat_query, mat_key, mat_value = again
    grad_out_rows = cotangent.reshape(row_count, model_width).astype(jnp.float32)
    grad_two, grad_gain_b, grad_shift_b = back_two(grad_out_rows)
    grad_second = grad_two.astype(low_type)
    grad_mat_down = inner_rows(active, grad_second)
    grad_vec_down = column_sum(grad_second)
    grad_hidden = back_gelu(times_back(grad_second, mat_down))[0].astype(low_type)
    grad_mat_up = inner_rows(first_low, grad_hidden)
    grad_vec_up = column_sum(grad_hidden)
    grad_first = grad_two + times_back(grad_hidden, mat_up)
    grad_one, grad_gain_a, grad_shift_a = back_one(grad_first)
    grad_branch = grad_one.astype(low_type)
    grad_mat_out = inner_rows(context_low, grad_branch)
    grad_vec_out = column_sum(grad_branch)
    grad_context = times_back(grad_branch, mat_out).astype(low_type)
    grad_heads = grad_context.reshape(seq_count, tok_count, head_count, head_size)
    row_delta = jnp.einsum("sqhe,sqhe->shq", grad_heads.astype(jnp.float32), context_heads)

    def block_grads(query_h, grad_h, log_t, delta, key_blk, value_blk):
        key_part = key_blk.reshape(seq_count, tok_count, head_count, head_size)
        value_part = value_blk.reshape(seq_count, tok_count, head_count, head_size)
        scores = jnp.einsum(
            "sqhe,skhe->shqk", query_h, key_part, preferred_element_type=jnp.float32
        )
        chances = jnp.exp(scores - log_t[..., None])
        value_grad = jnp.einsum(
            "shqk,sqhe->skhe", chances.astype(low_type), grad_h, preferred_element_type=jnp.float32
        )
        chance_grad = jnp.einsum(
            "sqhe,skhe->shqk", grad_h, value_part, preferred_element_type=jnp.float32
        )
        score_grad = (chances * (chance_grad - delta[..., None])).astype(low_type)
        query_grad = jnp.einsum(
            "shqk,skhe->sqhe", score_grad, key_part, preferred_element_type=jnp.float32
        )
        key_grad = jnp.einsum(
            "shqk,sqhe->skhe", score_grad, query_h, preferred_element_type=jnp.float32
        )
        return (
            query_grad,
            key_grad.reshape(seq_count, tok_count, model_width),
            value_grad.reshape(seq_count, tok_count, model_width),
        )

    zero_block = jnp.zeros((seq_count, tok_count, model_width), jnp.float32)
    zero_query = jnp.zeros((seq_count, tok_count, head_count, head_size), jnp.float32)

    def cycle_step(index, state):
        key_blk, value_blk, key_acc, value_acc, query_acc = state
        query_grad, key_grad, value_grad = block_grads(
            query_heads, grad_heads, log_total, row_delta, key_blk, value_blk
        )
        key_blk, value_blk = shifted((key_blk, value_blk), "ctx", 1)
        key_acc, value_acc = shifted((key_acc + key_grad, value_acc + value_grad), "ctx", 1)
        return (key_blk, value_blk, key_acc, value_acc, query_acc + query_grad)

    state = lax.fori_loop(
        0,
        lax.axis_size("ctx") - 1,
        cycle_step,
        (key_block, value_block, zero_block, zero_block, zero_query),
    )
    key_blk, value_blk, key_acc, value_acc, query_acc = state
    query_grad, key_grad, value_grad = block_grads(
        query_heads, grad_heads, log_total, row_delta, key_blk, value_blk
    )
    key_acc, value_acc = shifted((key_acc + key_grad, value_acc + value_grad), "ctx", 1)
    query_acc = query_acc + query_grad
    grad_query = query_acc.reshape(row_count, model_width).astype(low_type)
    grad_key = key_acc.reshape(row_count, model_width).astype(low_type)
    grad_value = value_acc.reshape(row_count, model_width).astype(low_type)
    grad_mat_query = inner_rows(tok_rows, grad_query) * scaling
    grad_vec_query = column_sum(grad_query) * scaling
    grad_mat_key = inner_rows(tok_rows, grad_key)
    grad_mat_value = inner_rows(tok_rows, grad_value)
    grad_vec_value = column_sum(grad_value)
    grad_in = (
        grad_one
        + times_back(grad_query, mat_query) * scaling
        + times_back(grad_key, mat_key)
        + times_back(grad_value, mat_value)
    )
    shares = (
        lax.psum_scatter(grad_mat_query, "fsdp", scatter_dimension=0, tiled=True),
        lax.psum_scatter(grad_vec_query, "fsdp", scatter_dimension=0, tiled=True),
        lax.psum_scatter(grad_mat_key, "fsdp", scatter_dimension=0, tiled=True),
        lax.psum_scatter(grad_mat_value, "fsdp", scatter_dimension=0, tiled=True),
        lax.psum_scatter(grad_vec_value, "fsdp", scatter_dimension=0, tiled=True),
        lax.psum_scatter(grad_mat_out, "fsdp", scatter_dimension=0, tiled=True),
        lax.psum_scatter(grad_vec_out, "fsdp", scatter_dimension=0, tiled=True),
        lax.psum_scatter(grad_gain_a, "fsdp", scatter_dimension=0, tiled=True),
        lax.psum_scatter(grad_shift_a, "fsdp", scatter_dimension=0, tiled=True),
        lax.psum_scatter(grad_mat_up, "fsdp", scatter_dimension=0, tiled=True),
        lax.psum_scatter(grad_vec_up, "fsdp", scatter_dimension=0, tiled=True),
        lax.psum_scatter(grad_mat_down, "fsdp", scatter_dimension=0, tiled=True),
        lax.psum_scatter(grad_vec_down, "fsdp", scatter_dimension=0, tiled=True),
        lax.psum_scatter(grad_gain_b, "fsdp", scatter_dimension=0, tiled=True),
        lax.psum_scatter(grad_shift_b, "fsdp", scatter_dimension=0, tiled=True),
    )
    totals = lax.psum(
        (
            shares[0],
            shares[1],
            shares[2],
            shares[3],
            shares[4],
            shares[5],
            shares[6],
            shares[7],
            shares[8],
            shares[9],
            shares[10],
            shares[11],
            shares[12],
            shares[13],
            shares[14],
        ),
        "ctx",
    )
    return (
        result.reshape(seq_count, tok_count, model_width).astype(low_type),
        grad_in.reshape(seq_count, tok_count, model_width),
        totals[0],
        totals[1],
        totals[2],
        totals[3],
        totals[4],
        totals[5],
        totals[6],
        totals[7],
        totals[8],
        totals[9],
        totals[10],
        totals[11],
        totals[12],
        totals[13],
        totals[14],
    )


def solution(mesh):
    return jax.shard_map(
        on_device,
        mesh=mesh,
        in_specs=(
            P("fsdp", "ctx", None),
            P("fsdp", None),
            P("fsdp"),
            P("fsdp", None),
            P("fsdp", None),
            P("fsdp"),
            P("fsdp", None),
            P("fsdp"),
            P("fsdp"),
            P("fsdp"),
            P("fsdp", None),
            P("fsdp"),
            P("fsdp", None),
            P("fsdp"),
            P("fsdp"),
            P("fsdp"),
            P("fsdp", "ctx", None),
        ),
        out_specs=(
            P("fsdp", "ctx", None),
            P("fsdp", "ctx", None),
            P("fsdp", None),
            P("fsdp"),
            P("fsdp", None),
            P("fsdp", None),
            P("fsdp"),
            P("fsdp", None),
            P("fsdp"),
            P("fsdp"),
            P("fsdp"),
            P("fsdp", None),
            P("fsdp"),
            P("fsdp", None),
            P("fsdp"),
            P("fsdp"),
            P("fsdp"),
        ),
        check_vma=False,
    )
```

profile of v0, /device:TPU:1, one launch (start us, length us, event | category | flops | bytes accessed | tf_op | source)
XLA Modules:
  0.0 2297.3 jit_solution(3564225922336867804)
XLA Ops:
  9.5 55.6 %all-gather.22.cloned.1.call-done = bf16[1024,1024]{1,0:T(8,128)(2,1)} async-done(((bf16[128,1024]{1,0:T(8,128)(2,1)}), bf16[1024,1024]{1,0:T(8,128)(2,1)}) %all-gather.22.cloned.1.call-update) | async-done | bytes 2097168 | tf_op jit(solution)/shard_map/all_gather | solution.py:67
  67.9 12.3 all-gather.3
  80.2 37.9 %all-gather.24.cloned.1.call-done = bf16[1024,1024]{1,0:T(8,128)(2,1)} async-done(((bf16[128,1024]{1,0:T(8,128)(2,1)}), bf16[1024,1024]{1,0:T(8,128)(2,1)}) %all-gather.24.cloned.1.call-update) | async-done | bytes 2097168 | tf_op jit(solution)/shard_map/all_gather | solution.py:68
  123.2 11.8 all-gather.2
  135.1 14.7 all-gather.4
  149.7 12.7 all-gather.5
  162.5 13.4 all-gather.6
  175.9 19.5 all-gather.7
  195.4 11.5 all-gather.8
  206.9 13.8 all-gather.9
  220.7 12.0 all-gather.10
  236.0 7.0 copy.60
  243.0 42.4 %all-gather.34.cloned.1.call-done = bf16[2048,1024]{1,0:T(8,128)(2,1)} async-done(((bf16[128,1024]{1,0:T(8,128)(2,1)}), bf16[2048,1024]{1,0:T(8,128)(2,1)}) %all-gather.34.cloned.1.call-update) | async-done | bytes 4194320 | tf_op jit(solution)/shard_map/all_gather | solution.py:115
  285.5 6.5 copy.61
  292.0 10.4 fusion.72
  302.4 8.2 fusion.11
  310.6 10.9 bitcast_convert_fusion
  321.6 15.0 all-gather.26.cloned.1.call-done
  338.9 166.9 %all-gather.28.cloned.1.call-done = bf16[1024,4096]{1,0:T(8,128)(2,1)} async-done(((bf16[128,4096]{1,0:T(8,128)(2,1)}), bf16[1024,4096]{1,0:T(8,128)(2,1)}) %all-gather.28.cloned.1.call-update) | async-done | bytes 8388624 | tf_op jit(solution)/shard_map/all_gather | solution.py:74
  505.9 9.6 multiply_convert_fusion
  515.4 161.5 %all-gather.30.cloned.1.call-done = bf16[4096,1024]{1,0:T(8,128)(2,1)} async-done(((bf16[512,1024]{1,0:T(8,128)(2,1)}), bf16[4096,1024]{1,0:T(8,128)(2,1)}) %all-gather.30.cloned.1.call-update) | async-done | bytes 8388624 | tf_op jit(solution)/shard_map/all_gather | solution.py:76
  676.9 4.9 fusion.74
  683.7 5.3 convert_reduce_fusion
  699.8 444.4 %while.19 = (s32[]{:T(128)}, bf16[1,128,1024]{1,2,0:T(8,128)(2,1)S(1)}, bf16[1,128,1024]{1,2,0:T(8,128)(2,1)}, f32[1,128,1024]{1,2,0:T(8,128)S(1)}, f32[1,128,10...) while((s32[]{:T(128)}, ...), condition=%wide.region_11.0_spmd.clone, body=%wide.region_10.0_spmd.clone.sunk | while | flops 169607168 | bytes 19153180 | solution.py:209
  710.6 35.3 %collective-permute-done = bf16[1,128,1024]{1,2,0:T(8,128)(2,1)S(1)} collective-permute-done((bf16[1,128,1024]{1,2,0:T(8,128)(2,1)S(1)}, bf16[1,128,1024]{1,2,0:T(8,128)(2,1)S(1)}, u32[]{:S(2)}, u32[]{:S(2)}) %collective-permute-start) | collective-permute-done | bytes 262176 | tf_op jit(solution)/shard_map/while/body/eval_jaxpr/ppermute | solution.py:15
  745.8 8.4 collective-permute-done.1
  765.1 39.4 %collective-permute-done = bf16[1,128,1024]{1,2,0:T(8,128)(2,1)S(1)} collective-permute-done((bf16[1,128,1024]{1,2,0:T(8,128)(2,1)S(1)}, bf16[1,128,1024]{1,2,0:T(8,128)(2,1)S(1)}, u32[]{:S(2)}, u32[]{:S(2)}) %collective-permute-start) | collective-permute-done | bytes 262176 | tf_op jit(solution)/shard_map/while/body/eval_jaxpr/ppermute | solution.py:15
  804.5 8.4 collective-permute-done.1
  824.6 10.4 collective-permute-done
  850.3 9.5 collective-permute-done
  876.1 8.6 collective-permute-done
  901.8 7.7 collective-permute-done
  920.7 4.5 collective-permute-start
  927.5 6.8 collective-permute-done
  946.0 5.0 collective-permute-start
  953.3 5.9 collective-permute-done
  971.7 5.0 collective-permute-start
  979.0 5.0 collective-permute-done
  997.4 5.0 collective-permute-start
  1023.2 5.0 collective-permute-start
  1030.5 5.4 collective-permute-done
  1048.9 5.0 collective-permute-start
  1056.3 6.6 collective-permute-done
  1069.8 4.9 collective-permute-start.3
  1074.7 5.0 collective-permute-start
  1082.0 7.8 collective-permute-done
  1095.0 5.4 collective-permute-start.3
  1100.4 5.0 collective-permute-start
  1107.7 9.0 collective-permute-done
  1121.7 4.5 collective-permute-start.3
  1126.2 5.0 collective-permute-start
  1133.5 10.2 collective-permute-done
  1150.3 21.3 collective-permute-done.4
  1175.9 9.4 collective-permute-done.5
  1189.2 8.1 fusion.77
  1198.6 8.2 fusion.66
  1206.9 54.3 %reduce-scatter.7.cloned.1.call-done = f32[128,1024]{0,1:T(8,128)} async-done(((f32[1024,1024]{0,1:T(8,128)}), f32[128,1024]{0,1:T(8,128)}) %reduce-scatter.7.cloned.1.call-update) | async-done | bytes 524304 | tf_op jit(solution)/shard_map/reduce_scatter | solution.py:236
  1261.2 94.4 %reduce-scatter.9.cloned.1.call-done = f32[128,1024]{0,1:T(8,128)} async-done(((f32[1024,1024]{0,1:T(8,128)}), f32[128,1024]{0,1:T(8,128)}) %reduce-scatter.9.cloned.1.call-update) | async-done | bytes 524304 | tf_op jit(solution)/shard_map/reduce_scatter | solution.py:238
  1355.6 93.5 %reduce-scatter.11.cloned.1.call-done = f32[128,1024]{0,1:T(8,128)} async-done(((f32[1024,1024]{0,1:T(8,128)}), f32[128,1024]{0,1:T(8,128)}) %reduce-scatter.11.cloned.1.call-update) | async-done | bytes 524304 | tf_op jit(solution)/shard_map/reduce_scatter | solution.py:239
  1449.1 329.0 %reduce-scatter.17.cloned.1.call-done = f32[512,1024]{1,0:T(8,128)} async-done(((f32[4096,1024]{1,0:T(8,128)}), f32[512,1024]{1,0:T(8,128)}) %reduce-scatter.17.cloned.1.call-update) | async-done | bytes 2097168 | tf_op jit(solution)/shard_map/reduce_scatter | solution.py:247
  1778.1 329.8 %reduce-scatter.15.cloned.1.call-done = f32[128,4096]{1,0:T(8,128)} async-done(((f32[1024,4096]{1,0:T(8,128)}), f32[128,4096]{1,0:T(8,128)}) %reduce-scatter.15.cloned.1.call-update) | async-done | bytes 2097168 | tf_op jit(solution)/shard_map/reduce_scatter | solution.py:245
  2114.0 29.6 %all-reduce.11 = (f32[1024]{0:T(1024)S(1)}, f32[1024]{0:T(1024)S(1)}, f32[1024]{0:T(1024)S(1)}, f32[1024]{0:T(1024)S(1)}, f32[1024]{0:T(1024)S(1)}, /*index=5*/f...) all-reduce(f32[1024]{0:T(1024)S(1)} %mul.208, ...), channel_id=5, replica_groups=mesh['ctx'=16,'fsdp'=8] {'fsdp'}, use_global_device_ids=true, to_apply=%region_15.0.clone | all-reduce | flops 12288 | bytes 98304
  2144.2 39.5 %all-reduce.9 = (f32[128]{0:T(128)}, f32[128]{0:T(128)}, f32[128]{0:T(128)}, f32[128]{0:T(128)}, f32[128]{0:T(128)}, /*index=5*/f32[512]{0:T(512)}, f32[128]{0:T(128)}, f32[128]{0:T(128)}, f32[128]{0:T(128)}) all-reduce(f32[128]{0:T(128)S(1)} %dynamic-slice.1, f32[128]{0:T(128)S(1)} %dynamic-slice.3, ...), channel_id=1, replica_groups=mesh['ctx'=16,'fsdp'=8] {'ctx'}, use_global_device_ids=true, to_apply=%region_16.0 | all-reduce | flops 1536 | bytes 12288 | tf_op jit(solution)/shard_map/psum | solution.py:252
  2187.0 93.7 %all-reduce.14.cloned.1.call-done = (f32[128,1024]{0,1:T(8,128)}, f32[128,1024]{0,1:T(8,128)}, f32[128,1024]{0,1:T(8,128)}, f32[128,1024]{1,0:T(8,128)}, f32[128,4096]{1,0:T(8,128)}, /*index=5*/f32[512,1024]{1,0:T(8,128)}) async-done(((f32[128,1024]{0,1:T(8,128)}, f32[128,1024]{0,1:T(8,128)}, f32[128,1024]{0,1:T(8,128)}, f32[128,1024]{1,0:T(8,128)}, f32[128,4096]{1,0:T(8,128)}, ...) | async-done | bytes 6291472 | tf_op jit(solution)/shard_map/psum | solution.py:252
  (431 shorter events, 262.1 us)
Async XLA Ops:
  7.2 57.8 %all-gather.22.cloned.1.call-start = ((), (), s32[]{:S(2)}) async-start(), calls=%async_computation.7 | async-start | bytes 2359296 | tf_op jit(solution)/shard_map/all_gather | solution.py:67
  7.9 110.2 %all-gather.24.cloned.1.call-start = ((), (), s32[]{:S(2)}) async-start(), calls=%async_computation.8 | async-start | bytes 2359296 | tf_op jit(solution)/shard_map/all_gather | solution.py:68
  8.7 224.0 %all-gather.20.cloned.1.call-start = ((), (), s32[]{:S(2)}) async-start(), calls=%async_computation.6 | async-start | bytes 2359296 | tf_op jit(solution)/shard_map/all_gather | solution.py:65
  9.4 226.5 %all-gather.32.cloned.1.call-start = ((), (), s32[]{:S(2)}) async-start(), calls=%async_computation.18 | async-start | bytes 4456448 | tf_op jit(solution)/shard_map/all_gather | solution.py:112
  67.9 217.6 %all-gather.34.cloned.1.call-start = ((), (), s32[]{:S(2)}) async-start(), calls=%async_computation.19 | async-start | bytes 4456448 | tf_op jit(solution)/shard_map/all_gather | solution.py:115
  121.1 215.5 %all-gather.26.cloned.1.call-start = ((), (), s32[]{:S(2)}) async-start(), calls=%async_computation.9 | async-start | bytes 2359296 | tf_op jit(solution)/shard_map/all_gather | solution.py:70
  121.6 384.2 %all-gather.28.cloned.1.call-start = ((), (), s32[]{:S(2)}) async-start(), calls=%async_computation.10 | async-start | bytes 9437184 | tf_op jit(solution)/shard_map/all_gather | solution.py:74
  122.4 554.5 %all-gather.30.cloned.1.call-start = ((), (), s32[]{:S(2)}) async-start(), calls=%async_computation.11 | async-start | bytes 9437184 | tf_op jit(solution)/shard_map/all_gather | solution.py:76
  123.2 1083.7 %reduce-scatter.13.cloned.1.call-start = ((), (), s32[]{:S(2)}) async-start(), calls=%async_computation.15 | async-start | bytes 4718592 | tf_op jit(solution)/shard_map/reduce_scatter | solution.py:241
  698.7 562.5 %reduce-scatter.7.cloned.1.call-start = ((), (), s32[]{:S(2)}) async-start(), calls=%async_computation.12 | async-start | bytes 4718592 | tf_op jit(solution)/shard_map/reduce_scatter | solution.py:236
  703.2 51.0 %collective-permute-start.2 = (f32[1,128,1024]{1,2,0:T(8,128)}, f32[1,128,1024]{1,2,0:T(8,128)S(1)}, u32[]{:S(2)}, u32[]{:S(2)}) collective-permute-start(f32[1,128,1024]{1,2,0:T(8,128)} %bitcast_add_fusion.6), channel_id=1, source_target_pairs={{120,0},{0,8},{8,16},{16,24},{24,32},{32,40},{40,48},{48,56},{56,6... | collective-permute-start | bytes 1572872 | tf_op jit(solution)/shard_map/while/body/eval_jaxpr/ppermute | solution.py:15
  707.4 46.9 %collective-permute-start.3 = (f32[1,128,1024]{1,2,0:T(8,128)}, f32[1,128,1024]{1,2,0:T(8,128)S(1)}, u32[]{:S(2)}, u32[]{:S(2)}) collective-permute-start(f32[1,128,1024]{1,2,0:T(8,128)} %bitcast_add_fusion.7), channel_id=1, source_target_pairs={{120,0},{0,8},{8,16},{16,24},{24,32},{32,40},{40,48},{48,56},{56,6... | collective-permute-start | bytes 1572872 | tf_op jit(solution)/shard_map/while/body/eval_jaxpr/ppermute | solution.py:15
  707.4 38.4 %collective-permute-start = (bf16[1,128,1024]{1,2,0:T(8,128)(2,1)S(1)}, bf16[1,128,1024]{1,2,0:T(8,128)(2,1)S(1)}, u32[]{:S(2)}, u32[]{:S(2)}) collective-permute-start(bf16[1,128,1024]{1,2,0:T(8,128)(2,1)S(1)} %copy.86), channel_id=1, source_target_pairs={{120,0},{0,8},{8,16},{16,24},{24,32},{32,40},{40,48},{48,56},{56,6... | collective-permute-start | bytes 786440 | tf_op jit(solution)/shard_map/while/body/eval_jaxpr/ppermute | solution.py:15
  709.3 45.0 %collective-permute-start.1 = (bf16[1,128,1024]{1,2,0:T(8,128)(2,1)S(1)}, bf16[1,128,1024]{1,2,0:T(8,128)(2,1)}, u32[]{:S(2)}, u32[]{:S(2)}) collective-permute-start(bf16[1,128,1024]{1,2,0:T(8,128)(2,1)S(1)} %copy.87), channel_id=1, source_target_pairs={{120,0},{0,8},{8,16},{16,24},{24,32},{32,40},{40,48},{48,56},{56,6... | collective-permute-start | bytes 786440 | tf_op jit(solution)/shard_map/while/body/eval_jaxpr/ppermute | solution.py:15
  757.4 55.5 %collective-permute-start.2 = (f32[1,128,1024]{1,2,0:T(8,128)}, f32[1,128,1024]{1,2,0:T(8,128)S(1)}, u32[]{:S(2)}, u32[]{:S(2)}) collective-permute-start(f32[1,128,1024]{1,2,0:T(8,128)} %bitcast_add_fusion.6), channel_id=1, source_target_pairs={{120,0},{0,8},{8,16},{16,24},{24,32},{32,40},{40,48},{48,56},{56,6... | collective-permute-start | bytes 1572872 | tf_op jit(solution)/shard_map/while/body/eval_jaxpr/ppermute | solution.py:15
  762.7 50.3 %collective-permute-start.3 = (f32[1,128,1024]{1,2,0:T(8,128)}, f32[1,128,1024]{1,2,0:T(8,128)S(1)}, u32[]{:S(2)}, u32[]{:S(2)}) collective-permute-start(f32[1,128,1024]{1,2,0:T(8,128)} %bitcast_add_fusion.7), channel_id=1, source_target_pairs={{120,0},{0,8},{8,16},{16,24},{24,32},{32,40},{40,48},{48,56},{56,6... | collective-permute-start | bytes 1572872 | tf_op jit(solution)/shard_map/while/body/eval_jaxpr/ppermute | solution.py:15
  762.7 41.9 %collective-permute-start = (bf16[1,128,1024]{1,2,0:T(8,128)(2,1)S(1)}, bf16[1,128,1024]{1,2,0:T(8,128)(2,1)S(1)}, u32[]{:S(2)}, u32[]{:S(2)}) collective-permute-start(bf16[1,128,1024]{1,2,0:T(8,128)(2,1)S(1)} %copy.86), channel_id=1, source_target_pairs={{120,0},{0,8},{8,16},{16,24},{24,32},{32,40},{40,48},{48,56},{56,6... | collective-permute-start | bytes 786440 | tf_op jit(solution)/shard_map/while/body/eval_jaxpr/ppermute | solution.py:15
  762.7 50.3 %collective-permute-start.1 = (bf16[1,128,1024]{1,2,0:T(8,128)(2,1)S(1)}, bf16[1,128,1024]{1,2,0:T(8,128)(2,1)}, u32[]{:S(2)}, u32[]{:S(2)}) collective-permute-start(bf16[1,128,1024]{1,2,0:T(8,128)(2,1)S(1)} %copy.87), channel_id=1, source_target_pairs={{120,0},{0,8},{8,16},{16,24},{24,32},{32,40},{40,48},{48,56},{56,6... | collective-permute-start | bytes 786440 | tf_op jit(solution)/shard_map/while/body/eval_jaxpr/ppermute | solution.py:15
  816.1 21.7 collective-permute-start.2
  821.4 16.4 collective-permute-start.3
  821.4 13.6 collective-permute-start
  822.2 15.6 collective-permute-start.1
  841.0 21.7 collective-permute-start.2
  846.2 16.4 collective-permute-start.3
  846.2 13.6 collective-permute-start
  848.0 14.7 collective-permute-start.1
  865.8 21.7 collective-permute-start.2
  871.1 16.4 collective-permute-start.3
  871.1 13.6 collective-permute-start
  873.7 13.8 collective-permute-start.1
  890.7 21.7 collective-permute-start.2
  895.9 16.4 collective-permute-start.3
  895.9 13.6 collective-permute-start
  899.5 12.9 collective-permute-start.1
  915.5 21.7 collective-permute-start.2
  920.7 16.4 collective-permute-start.3
  920.7 13.6 collective-permute-start
  940.3 21.7 collective-permute-start.2
  945.6 16.4 collective-permute-start.3
  946.0 13.2 collective-permute-start
  965.2 21.7 collective-permute-start.2
  970.4 16.4 collective-permute-start.3
  990.0 21.7 collective-permute-start.2
  995.3 16.4 collective-permute-start.3
  1014.9 21.7 collective-permute-start.2
  1020.1 16.4 collective-permute-start.3
  1039.7 23.3 %collective-permute-start.2 = (f32[1,128,1024]{1,2,0:T(8,128)}, f32[1,128,1024]{1,2,0:T(8,128)S(1)}, u32[]{:S(2)}, u32[]{:S(2)}) collective-permute-start(f32[1,128,1024]{1,2,0:T(8,128)} %bitcast_add_fusion.6), channel_id=1, source_target_pairs={{120,0},{0,8},{8,16},{16,24},{24,32},{32,40},{40,48},{48,56},{56,6... | collective-permute-start | bytes 1572872 | tf_op jit(solution)/shard_map/while/body/eval_jaxpr/ppermute | solution.py:15
  1045.0 18.5 collective-permute-start.3
  1048.9 13.9 collective-permute-start
  1066.6 23.4 %collective-permute-start.2 = (f32[1,128,1024]{1,2,0:T(8,128)}, f32[1,128,1024]{1,2,0:T(8,128)S(1)}, u32[]{:S(2)}, u32[]{:S(2)}) collective-permute-start(f32[1,128,1024]{1,2,0:T(8,128)} %bitcast_add_fusion.6), channel_id=1, source_target_pairs={{120,0},{0,8},{8,16},{16,24},{24,32},{32,40},{40,48},{48,56},{56,6... | collective-permute-start | bytes 1572872 | tf_op jit(solution)/shard_map/while/body/eval_jaxpr/ppermute | solution.py:15
  1069.8 20.6 collective-permute-start.3
  1074.7 15.1 collective-permute-start
  1093.6 23.4 %collective-permute-start.2 = (f32[1,128,1024]{1,2,0:T(8,128)}, f32[1,128,1024]{1,2,0:T(8,128)S(1)}, u32[]{:S(2)}, u32[]{:S(2)}) collective-permute-start(f32[1,128,1024]{1,2,0:T(8,128)} %bitcast_add_fusion.6), channel_id=1, source_target_pairs={{120,0},{0,8},{8,16},{16,24},{24,32},{32,40},{40,48},{48,56},{56,6... | collective-permute-start | bytes 1572872 | tf_op jit(solution)/shard_map/while/body/eval_jaxpr/ppermute | solution.py:15
  1095.0 22.3 collective-permute-start.3
  1100.4 16.3 collective-permute-start
  1120.5 23.4 %collective-permute-start.2 = (f32[1,128,1024]{1,2,0:T(8,128)}, f32[1,128,1024]{1,2,0:T(8,128)S(1)}, u32[]{:S(2)}, u32[]{:S(2)}) collective-permute-start(f32[1,128,1024]{1,2,0:T(8,128)} %bitcast_add_fusion.6), channel_id=1, source_target_pairs={{120,0},{0,8},{8,16},{16,24},{24,32},{32,40},{40,48},{48,56},{56,6... | collective-permute-start | bytes 1572872 | tf_op jit(solution)/shard_map/while/body/eval_jaxpr/ppermute | solution.py:15
  1121.7 22.6 collective-permute-start.3
  1126.2 17.5 collective-permute-start
  1149.9 205.7 %reduce-scatter.9.cloned.1.call-start = ((), (), s32[]{:S(2)}) async-start(), calls=%async_computation.13 | async-start | bytes 4718592 | tf_op jit(solution)/shard_map/reduce_scatter | solution.py:238
  1150.3 21.4 collective-permute-start.4
  1174.3 274.8 %reduce-scatter.11.cloned.1.call-start = ((), (), s32[]{:S(2)}) async-start(), calls=%async_computation.14 | async-start | bytes 4718592 | tf_op jit(solution)/shard_map/reduce_scatter | solution.py:239
  1188.0 590.1 %reduce-scatter.17.cloned.1.call-start = ((), (), s32[]{:S(2)}) async-start(), calls=%async_computation.17 | async-start | bytes 18874368 | tf_op jit(solution)/shard_map/reduce_scatter | solution.py:247
  1197.4 910.6 %reduce-scatter.15.cloned.1.call-start = ((), (), s32[]{:S(2)}) async-start(), calls=%async_computation.16 | async-start | bytes 18874368 | tf_op jit(solution)/shard_map/reduce_scatter | solution.py:245
  1206.8 1074.0 %all-reduce.14.cloned.1.call-start = ((), (), s32[]{:S(2)}) async-start(), calls=%async_computation.20 | async-start | bytes 12582912 | tf_op jit(solution)/shard_map/psum | solution.py:252
  (59 other events, 1436.4 us)
Sparse Core Ops, SparseCore 0:
  9.7 55.2 all-gather.21
  66.7 51.4 all-gather.23
  119.8 51.6 all-gather.19
  174.4 55.0 all-gather.31
  232.4 53.0 all-gather.33
  286.9 49.5 all-gather.25
  338.2 167.6 all-gather.27
  507.5 169.3 all-gather.29
  698.8 123.2 reduce-scatter.12
  1150.0 111.1 reduce-scatter.6
  1263.6 91.9 reduce-scatter.8
  1357.8 91.2 reduce-scatter.10
  1451.6 326.4 reduce-scatter.16
  1780.4 327.4 reduce-scatter.14
  2110.8 169.9 all-reduce.13
where the time goes:
time: 2300 us
  waiting for transfers between devices  1720 us (75%)
  blocking collectives  191 us (8%)
  matrix products  149 us (6%)
  starting transfers between devices  133 us (6%)
  local copies, waits for them, and re-layouts  47.8 us (2%)
  other arithmetic  37.2 us (2%)
    reduce_scatter x1, waiting for transfers between devices, on_device(): lax.psum_scatter(grad_mat_up, 'fsdp', scatter_dimension=0, tiled=True)  330 us
    reduce_scatter x1, waiting for transfers between devices, on_device(): lax.psum_scatter(grad_mat_down, 'fsdp', scatter_dimension=0, tiled=True)  329 us
    ppermute x62, waiting for transfers between devices, shifted(): return lax.ppermute(block, axis, route)  245 us
    all_gather x1, waiting for transfers between devices, on_device(): lax.all_gather(w_up, 'fsdp', axis=0, tiled=True)  167 us
    all_gather x1, waiting for transfers between devices, on_device(): lax.all_gather(w_down, 'fsdp', axis=0, tiled=True)  161 us
    ppermute x62, starting transfers between devices, shifted(): return lax.ppermute(block, axis, route)  132 us
    reduce_scatter x1, waiting for transfers between devices, on_device(): lax.psum_scatter(grad_mat_key, 'fsdp', scatter_dimension=0, tiled=True)  94.4 us
    psum x1, waiting for transfers between devices, on_device(): lax.psum((shares[0], shares[1], shares[2], shares[3], shares[4], shares[5...  93.7 us
  transfers between devices with their start and end apart: 77, of which 48 were waited for; matrix products, arithmetic and copies ran while one was open for 9% of the time, Pallas kernels for 0%

commit v1 on v0

v1 whole, which is shorter than its diff:
```python
import functools

import jax
import jax.numpy as jnp
from jax import lax
from jax.experimental import pallas as pl
from jax.experimental.pallas import tpu as pltpu
from jax.sharding import PartitionSpec as P

EPSILON = 1e-05
LOW = jnp.bfloat16
F32 = jnp.float32
WIDTH = 1024
HEAD = 64
ROWS = 128
LENGTH = 2048
CHUNK = 512
QUERIES = 256
SAME_CORE = [list(range(0, 16, 2)), list(range(1, 16, 2))]
SAME_LOW = [list(range(0, 8, 2)), list(range(1, 8, 2))]
VMEM_LIMIT = 50 * 1024 * 1024


def over_ctx(block, y=0, x=0, core=0):
    route = [
        (i, (((i >> 2) + y) % 4) * 4 + (((i >> 1) & 1) ^ x) * 2 + ((i & 1) ^ core))
        for i in range(16)
    ]
    return lax.ppermute(block, "ctx", route)


def over_fsdp(block, z=0, x=0):
    route = [(i, (((i >> 1) + z) % 4) * 2 + ((i & 1) ^ x)) for i in range(8)]
    return lax.ppermute(block, "fsdp", route)


def dims(matrix, other, left, right):
    return lax.dot_general(
        matrix, other, (((left,), (right,)), ((), ())), preferred_element_type=F32
    )


def dot(matrix, other):
    return dims(matrix, other, 1, 0)


def split_low(value):
    high = value.astype(LOW)
    return high, (value - high.astype(F32)).astype(LOW)


def norm_forward(hidden, gain, shift):
    center = hidden - jnp.mean(hidden, axis=-1, keepdims=True)
    scale = lax.rsqrt(jnp.mean(center * center, axis=-1, keepdims=True) + EPSILON)
    unit = center * scale
    return unit * gain + shift, unit, scale


def norm_backward(grad, unit, scale, gain):
    inner = grad * gain
    mean_inner = jnp.mean(inner, axis=-1, keepdims=True)
    mean_unit = jnp.mean(inner * unit, axis=-1, keepdims=True)
    back = scale * (inner - mean_inner - unit * mean_unit)
    return back, jnp.sum(grad * unit, axis=0), jnp.sum(grad, axis=0)


def forward_kernel(order, *refs):
    parts = refs[:8]
    w_ref, bias_q, bias_v, qkv, rows, mixed_low, mixed, total, held = refs[8:]
    weight = jnp.concatenate([w_ref[f, : 3 * HEAD, :] for f in range(8)], axis=1)
    for index, part in enumerate(parts):
        span = slice(index * QUERIES, (index + 1) * QUERIES)
        product = dims(weight, part[...], 1, 1)
        query = (product[:HEAD] + bias_q[...]) * (HEAD**-0.5)
        value = product[2 * HEAD :] + bias_v[...]
        pair = jnp.concatenate([product[HEAD : 2 * HEAD], value], axis=0)
        qkv[:HEAD, span] = query.astype(LOW)
        qkv[HEAD:, span] = pair.astype(LOW)
        rows[span, :] = pair.T.astype(LOW)

    def step(index, carry):
        span = pl.ds(pl.multiple_of(index * QUERIES, QUERIES), QUERIES)
        query = qkv[:HEAD, span]
        padded = jnp.concatenate([query, jnp.zeros_like(query)], axis=0)
        peak = None
        for at in range(0, LENGTH, CHUNK):
            scores = dot(rows[at : at + CHUNK, :], padded)
            held[at : at + CHUNK, :] = scores
            top = jnp.max(scores, axis=0, keepdims=True)
            peak = top if peak is None else jnp.maximum(peak, top)
        weight_sum = jnp.zeros((1, QUERIES), F32)
        acc = jnp.zeros((HEAD, QUERIES), F32)
        for at in range(0, LENGTH, CHUNK):
            weights = jnp.exp(held[at : at + CHUNK, :] - peak)
            weight_sum += jnp.sum(weights, axis=0, keepdims=True)
            acc += dot(qkv[2 * HEAD :, at : at + CHUNK], weights.astype(LOW))
        acc = acc / weight_sum
        mixed[:, span] = acc
        total[:, span] = peak + jnp.log(weight_sum)
        mixed_low[order[2 * index]] = acc[:, :ROWS].astype(LOW)
        mixed_low[order[2 * index + 1]] = acc[:, ROWS:].astype(LOW)
        return carry

    lax.fori_loop(0, LENGTH // QUERIES, step, 0)


def backward_kernel(order, grad_ref, qkv, rows, mixed, total, sent, kept, key_acc, value_acc):
    key_acc[...] = jnp.zeros_like(key_acc)
    value_acc[...] = jnp.zeros_like(value_acc)

    def step(index, carry):
        span = pl.ds(pl.multiple_of(index * QUERIES, QUERIES), QUERIES)
        first, second = order[2 * index], order[2 * index + 1]
        query = qkv[:HEAD, span]
        grad = jnp.concatenate([grad_ref[first], grad_ref[second]], axis=1)
        delta = jnp.sum(grad.astype(F32) * mixed[:, span], axis=0, keepdims=True)
        log_total = total[:, span]
        query_pad = jnp.concatenate([query, jnp.zeros_like(query)], axis=0)
        grad_pad = jnp.concatenate([jnp.zeros_like(grad), grad], axis=0)
        query_grad = jnp.zeros((HEAD, QUERIES), F32)
        for at in range(0, LENGTH, CHUNK):
            block = rows[at : at + CHUNK, :]
            chances = jnp.exp(dot(block, query_pad) - log_total)
            chance_grad = dot(block, grad_pad)
            score_grad = (chances * (chance_grad - delta)).astype(LOW)
            value_acc[:, at : at + CHUNK] += dims(grad, chances.astype(LOW), 1, 1)
            key_acc[:, at : at + CHUNK] += dims(query, score_grad, 1, 1)
            query_grad += dot(qkv[HEAD : 2 * HEAD, at : at + CHUNK], score_grad)
        low = query_grad.astype(LOW)
        kept[:HEAD, span] = low
        sent[first, :HEAD, :] = low[:, :ROWS]
        sent[second, :HEAD, :] = low[:, ROWS:]
        return carry

    lax.fori_loop(0, LENGTH // QUERIES, step, 0)
    kept[HEAD : 2 * HEAD, :] = key_acc[...].astype(LOW)
    kept[2 * HEAD :, :] = value_acc[...].astype(LOW)
    for index in range(LENGTH // ROWS):
        sent[order[index], HEAD:, :] = kept[HEAD:, index * ROWS : (index + 1) * ROWS]


def projection_kernel(grads, *refs):
    parts, out = refs[:8], refs[8]
    acc = None
    for index, part in enumerate(parts):
        term = dot(grads[:, index * QUERIES : (index + 1) * QUERIES], part[...])
        acc = term if acc is None else acc + term
    sums = dims(jnp.ones((8, LENGTH), LOW), grads[...], 1, 1)[:1]
    sums = jnp.concatenate([sums, jnp.zeros((1, HEAD), F32)], axis=1)
    high, rest = split_low(sums)
    tail = jnp.concatenate(
        [
            high.astype(F32)[:, :ROWS],
            high.astype(F32)[:, ROWS:],
            rest.astype(F32)[:, :ROWS],
            rest.astype(F32)[:, ROWS:],
            jnp.zeros((12, ROWS), F32),
        ],
        axis=0,
    ).astype(LOW)
    for index in range(8):
        out[index, : 3 * HEAD, :] = acc[:, index * ROWS : (index + 1) * ROWS].astype(LOW)
        out[index, 3 * HEAD :, :] = tail


def call(kernel, outs, scratch, flops, moved, *operands):
    in_specs = [pl.BlockSpec(memory_space=pltpu.SMEM if operand.dtype == jnp.int32 else pltpu.VMEM) for operand in operands]
    return pl.pallas_call(
        kernel,
        out_shape=[jax.ShapeDtypeStruct(shape, dtype) for shape, dtype in outs],
        in_specs=in_specs,
        out_specs=[pl.BlockSpec(memory_space=pltpu.VMEM)] * len(outs),
        scratch_shapes=scratch,
        compiler_params=pltpu.CompilerParams(vmem_limit_bytes=VMEM_LIMIT),
        cost_estimate=pl.CostEstimate(flops=flops, bytes_accessed=moved, transcendentals=0),
    )(*operands)


def on_device(
    inputs,
    w_query,
    b_query,
    w_key,
    w_value,
    b_value,
    w_out,
    b_out,
    gain_one,
    shift_one,
    w_up,
    b_up,
    w_down,
    b_down,
    gain_two,
    shift_two,
    cotangent,
):
    ctx, fsdp = lax.axis_index("ctx"), lax.axis_index("fsdp")
    core, x_hi, y = ctx & 1, (ctx >> 1) & 1, ctx >> 2
    x_lo, z = fsdp & 1, fsdp >> 1

    own = inputs.reshape(ROWS, WIDTH)
    pair = jnp.concatenate([own, over_ctx(own, x=1)], axis=0)
    near = [pair] + [over_ctx(pair, y=k) for k in (1, 2, 3)]
    parts = near + [over_ctx(part, core=1) for part in near]
    order = jnp.stack(
        [
            ((y - k) % 4) * 4 + (x_hi ^ j) * 2 + (core ^ s)
            for s in range(2)
            for k in range(4)
            for j in range(2)
        ]
    ).astype(jnp.int32)

    columns = [
        lax.dynamic_slice(w, (0, ctx * HEAD), (ROWS, HEAD)).T for w in (w_query, w_key, w_value)
    ]
    vectors = jnp.concatenate(
        [
            jnp.stack([b_query, b_value, b_out, gain_one, shift_one, b_down, gain_two, shift_two]),
            b_up.reshape(4, ROWS),
            jnp.zeros((4, ROWS), LOW),
        ]
    )
    message = jnp.concatenate(columns + [vectors], axis=0)
    heads = lax.all_to_all(
        jnp.broadcast_to(message[None], (8,) + message.shape), "fsdp", 0, 0, tiled=True
    )
    vecs = heads[:, 3 * HEAD :, :].astype(F32)

    def whole(index):
        return vecs[:, index, :].reshape(WIDTH)

    vec_query, vec_value, vec_out, gain_a, shift_a, vec_down, gain_b, shift_b = (
        whole(index) for index in range(8)
    )
    vec_up = lax.dynamic_slice(
        vecs[:, 8:12, :].reshape(8, 512), (0, core * 256), (8, 256)
    ).reshape(2048)
    bias_q = lax.dynamic_slice(vec_query, (ctx * HEAD,), (HEAD,)).reshape(HEAD, 1)
    bias_v = lax.dynamic_slice(vec_value, (ctx * HEAD,), (HEAD,)).reshape(HEAD, 1)

    half_out = lax.dynamic_slice(w_out, (core * 64, 0), (64, WIDTH))
    half_up = lax.dynamic_slice(
        w_up.reshape(ROWS, 8, 512), (0, 0, core * 256), (ROWS, 8, 256)
    ).reshape(ROWS, 2048)
    half_down = lax.dynamic_slice(w_down, (core * 256, 0), (256, WIDTH))
    half_in = [lax.dynamic_slice(w, (core * 64, 0), (64, WIDTH)) for w in (w_query, w_key, w_value)]
    packed = jnp.concatenate([half_out, half_up[:, :WIDTH], half_up[:, WIDTH:], half_down], axis=0)
    packed_in = jnp.concatenate(half_in, axis=0)

    def gather(block):
        other = over_fsdp(block, x=1)
        found = [(0, 0, block), (0, 1, other)]
        for k in (1, 3, 2):
            found.append((k, 0, over_fsdp(block, z=k)))
            found.append((k, 1, over_fsdp(other, z=k)))
        return [(((z - k) % 4) * 2 + (x_lo ^ j), part) for k, j, part in found]

    def place(found, low, high):
        size = high - low
        held = jnp.zeros((8, size, WIDTH), LOW)
        for at, part in found:
            held = lax.dynamic_update_slice(held, part[None, low:high], (at, 0, 0))
        return held

    found = gather(packed)
    mat_out = place(found, 0, 64)
    up_left = place(found, 64, 192).reshape(WIDTH, WIDTH)
    up_right = place(found, 192, 320).reshape(WIDTH, WIDTH)
    mat_down = place(found, 320, 576).reshape(2048, WIDTH)
    found_in = gather(packed_in)
    mat_in = place(found_in, 0, 192)

    def both_halves(mine):
        theirs = over_ctx(mine, core=1)
        return jnp.where(core == 0, mine, theirs), jnp.where(core == 0, theirs, mine)

    mat_out = jnp.stack(both_halves(mat_out), axis=1).reshape(WIDTH, WIDTH)
    mat_in = jnp.stack(both_halves(mat_in.reshape(8, 3, 64, WIDTH)), axis=2)
    mat_query, mat_key, mat_value = (mat_in[:, i].reshape(WIDTH, WIDTH) for i in range(3))

    qkv, rows, mixed_low, mixed, total = call(
        forward_kernel,
        [
            ((3 * HEAD, LENGTH), LOW),
            ((LENGTH, 2 * HEAD), LOW),
            ((16, HEAD, ROWS), LOW),
            ((HEAD, LENGTH), F32),
            ((1, LENGTH), F32),
        ],
        [pltpu.VMEM((LENGTH, QUERIES), F32)],
        10**10,
        10**7,
        order,
        *parts,
        heads,
        bias_q,
        bias_v,
    )
    context = lax.all_to_all(mixed_low, "ctx", 0, 0, tiled=True).reshape(WIDTH, ROWS)
    branch = dims(context, mat_out, 0, 0) + vec_out
    first, unit_one, scale_one = norm_forward(own.astype(F32) + branch, gain_a, shift_a)
    first_low = first.astype(LOW)
    first_two = jnp.concatenate([first_low, over_ctx(first_low, core=1)], axis=0)
    hidden = jnp.concatenate([dot(first_two, up_left), dot(first_two, up_right)], axis=1) + vec_up
    gate = 0.5 * (1.0 + lax.erf(hidden * (0.5**0.5)))
    slope = gate + hidden * jnp.exp(-0.5 * hidden * hidden) * 0.3989422804014327
    active = (hidden * gate).astype(LOW)
    second = dot(active, mat_down)
    second = second[:ROWS] + over_ctx(second[ROWS:], core=1) + vec_down
    result, unit_two, scale_two = norm_forward(first + second, gain_b, shift_b)

    grad_out = cotangent.reshape(ROWS, WIDTH).astype(F32)
    grad_two, grad_gain_b, grad_shift_b = norm_backward(grad_out, unit_two, scale_two, gain_b)
    grad_second = grad_two.astype(LOW)
    grad_vec_down = jnp.sum(grad_second.astype(F32), axis=0)
    second_two = jnp.concatenate([grad_second, over_ctx(grad_second, core=1)], axis=0)
    grad_hidden = (slope * dims(second_two, mat_down, 1, 1)).astype(LOW)
    grad_vec_up = jnp.sum(grad_hidden.astype(F32), axis=0)
    grad_first = dims(grad_hidden[:, :WIDTH], up_left, 1, 1) + dims(
        grad_hidden[:, WIDTH:], up_right, 1, 1
    )
    grad_first = grad_two + grad_first[:ROWS] + over_ctx(grad_first[ROWS:], core=1)
    grad_one, grad_gain_a, grad_shift_a = norm_backward(grad_first, unit_one, scale_one, gain_a)
    grad_branch = grad_one.astype(LOW)
    grad_vec_out = jnp.sum(grad_branch.astype(F32), axis=0)
    grad_context = dims(mat_out, grad_branch, 1, 1).astype(LOW).reshape(16, HEAD, ROWS)
    grad_heads = lax.all_to_all(grad_context, "ctx", 0, 0, tiled=True)
    sent, kept = call(
        backward_kernel,
        [((16, 3 * HEAD, ROWS), LOW), ((3 * HEAD, LENGTH), LOW)],
        [pltpu.VMEM((HEAD, LENGTH), F32), pltpu.VMEM((HEAD, LENGTH), F32)],
        10**10,
        10**7,
        order,
        grad_heads,
        qkv,
        rows,
        mixed,
        total,
    )
    back = lax.all_to_all(sent, "ctx", 0, 0, tiled=True)
    grad_in = grad_one + (
        dims(back[:, :HEAD].reshape(WIDTH, ROWS), mat_query, 0, 1) * (HEAD**-0.5)
        + dims(back[:, HEAD : 2 * HEAD].reshape(WIDTH, ROWS), mat_key, 0, 1)
        + dims(back[:, 2 * HEAD :].reshape(WIDTH, ROWS), mat_value, 0, 1)
    )

    (pieces,) = call(
        projection_kernel, [((8, 208, ROWS), LOW)], [], 10**9, 10**7, kept, *parts
    )
    pieces = jnp.sum(lax.all_to_all(pieces, "fsdp", 0, 0, tiled=True).astype(F32), axis=0)
    sums = jnp.concatenate(split_low(pieces[192:194] + pieces[194:196]), axis=0)
    message = jnp.concatenate([pieces[:192].astype(LOW), sums, jnp.zeros((12, ROWS), LOW)], axis=0)
    shared = lax.all_to_all(
        jnp.broadcast_to(message[None], (16,) + message.shape), "ctx", 0, 0, tiled=True
    ).astype(F32)
    grad_mat_query = shared[:, :HEAD].reshape(WIDTH, ROWS).T * (HEAD**-0.5)
    grad_mat_key = shared[:, HEAD : 2 * HEAD].reshape(WIDTH, ROWS).T
    grad_mat_value = shared[:, 2 * HEAD : 3 * HEAD].reshape(WIDTH, ROWS).T
    vec_sums = shared[:, 192:194] + shared[:, 194:196]
    mine = lax.dynamic_slice(vec_sums, (fsdp * 2, 0, 0), (2, 2, ROWS))
    grad_vec_query = mine[:, 0, :HEAD].reshape(ROWS) * (HEAD**-0.5)
    grad_vec_value = mine[:, 1, :HEAD].reshape(ROWS)

    def to_quarters(block, axis):
        size = block.shape[axis] // 4

        def quarter(index):
            return lax.dynamic_slice_in_dim(block, index * size, size, axis)

        return [quarter(z)] + [over_fsdp(quarter((z + k) % 4), z=k) for k in (1, 2, 3)]

    def from_all(block):
        return [block] + [over_fsdp(block, z=k) for k in (1, 2, 3)]

    def tokens(block):
        mine = jnp.stack(from_all(block))
        return jnp.stack([mine, over_ctx(mine, core=1)], axis=1).reshape(8 * ROWS, -1)

    active_z = jnp.concatenate(to_quarters(active, 1), axis=0)
    first_z = tokens(first_low)
    second_z = tokens(grad_second)
    hidden_z = jnp.concatenate(to_quarters(grad_hidden, 1), axis=0)
    context_z = jnp.concatenate(to_quarters(context, 0), axis=1)
    branch_z = jnp.concatenate(from_all(grad_branch), axis=0)
    down = dims(active_z, second_z, 0, 0).reshape(2, 256, WIDTH)
    up = dims(first_z, hidden_z, 0, 0).reshape(4, 2, ROWS, 512)
    out = dot(context_z, branch_z).reshape(2, 2, 64, WIDTH)

    def pick(block, index, axis):
        return lax.dynamic_index_in_dim(block, index, axis, keepdims=False)

    out = pick(out, core, 1) + over_ctx(pick(out, 1 - core, 1).astype(LOW), core=1).astype(F32)

    def wide(block):
        return jnp.concatenate([block[:, :2], block[:, 2:]], axis=-1).reshape(8, 32, WIDTH)

    def bundle(index):
        rows_up = pick(up, index, 1).reshape(4, 8, 16, 512).transpose(1, 0, 2, 3)
        return jnp.concatenate(
            [
                pick(down, index, 0).reshape(8, 32, WIDTH),
                wide(rows_up),
                pick(out, index, 0).reshape(8, 8, WIDTH),
            ],
            axis=1,
        )

    summed = bundle(x_lo) + over_fsdp(bundle(1 - x_lo).astype(LOW), x=1).astype(F32)
    summed = jnp.sum(
        lax.all_to_all(
            summed.astype(LOW), "ctx", 0, 0, axis_index_groups=SAME_CORE, tiled=True
        ).astype(F32),
        axis=0,
    ).astype(LOW)
    piece = summed[32:64].reshape(2, 16, WIDTH)
    piece = jnp.concatenate([piece[:, :, :512], piece[:, :, 512:]], axis=0)
    piece = lax.all_to_all(piece, "fsdp", 0, 0, axis_index_groups=SAME_LOW, tiled=True)
    piece = jnp.concatenate([piece[:2], piece[2:]], axis=-1).reshape(32, WIDTH)
    message = jnp.concatenate([summed[:32], piece, summed[64:]], axis=0)
    shared = lax.all_to_all(
        jnp.broadcast_to(message[None], (8, 72, WIDTH)),
        "ctx",
        0,
        0,
        axis_index_groups=SAME_CORE,
        tiled=True,
    )
    shared = jnp.stack(both_halves(shared)).astype(F32)
    grad_mat_down = shared[:, :, :32].reshape(512, WIDTH)
    grad_mat_out = shared[:, :, 64:].reshape(ROWS, WIDTH)
    grad_mat_up = (
        shared[:, :, 32:64]
        .reshape(2, 8, 2, 16, 2, 2, 256)
        .transpose(1, 3, 4, 2, 5, 0, 6)
        .reshape(ROWS, 4096)
    )

    halves = jnp.zeros((8, 2, 256), F32)
    halves = lax.dynamic_update_slice(halves, grad_vec_up.reshape(8, 1, 256), (0, core, 0))
    vector_grads = jnp.concatenate(
        [
            jnp.stack(
                [grad_vec_out, grad_gain_a, grad_shift_a, grad_vec_down, grad_gain_b, grad_shift_b]
            )
            .reshape(6, 8, ROWS)
            .transpose(1, 0, 2),
            halves.reshape(8, 4, ROWS),
        ],
        axis=1,
    )
    vector_grads = lax.psum(vector_grads, ("ctx", "fsdp"))
    vector_grads = pick(vector_grads, fsdp, 0)

    return (
        result.reshape(1, ROWS, WIDTH).astype(LOW),
        grad_in.reshape(1, ROWS, WIDTH),
        grad_mat_query,
        grad_vec_query,
        grad_mat_key,
        grad_mat_value,
        grad_vec_value,
        grad_mat_out,
        vector_grads[0],
        vector_grads[1],
        vector_grads[2],
        grad_mat_up,
        vector_grads[6:10].reshape(512),
        grad_mat_down,
        vector_grads[3],
        vector_grads[4],
        vector_grads[5],
    )


def solution(mesh):
    tokens, matrix, vector = P("fsdp", "ctx", None), P("fsdp", None), P("fsdp")
    return jax.shard_map(
        on_device,
        mesh=mesh,
        in_specs=(
            tokens,
            matrix,
            vector,
            matrix,
            matrix,
            vector,
            matrix,
            vector,
            vector,
            vector,
            matrix,
            vector,
            matrix,
            vector,
            vector,
            vector,
            tokens,
        ),
        out_specs=(
            tokens,
            tokens,
            matrix,
            vector,
            matrix,
            matrix,
            vector,
            matrix,
            vector,
            vector,
            vector,
            matrix,
            vector,
            matrix,
            vector,
            vector,
            vector,
        ),
        check_vma=False,
    )
```

time: 2300 us -> 574 us (0.25)
  waiting for transfers between devices: 1720 us -> 133 us
  blocking collectives: 191 us -> 66.2 us
  matrix products: 149 us -> 32.3 us
  local copies, waits for them, and re-layouts: 47.8 us -> 112 us
  Pallas kernels: 0 us -> 31.7 us
    reduce_scatter x6 -> x0, waiting for transfers between devices: 901 us -> none  [the longest x1 330 us: on_device(): lax.psum_scatter(grad_mat_up, 'fsdp', scatter_dimension=0, tiled=True)]
    all_gather x8 -> x0, waiting for transfers between devices: 479 us -> none  [the longest x1 167 us: on_device(): lax.all_gather(w_up, 'fsdp', axis=0, tiled=True)]
    ppermute x62 -> x51, waiting for transfers between devices: 245 us -> 101 us  [the longest x33 92 us: over_fsdp(): return lax.ppermute(block, 'fsdp', route)]
    all_gather x9 -> x0, blocking collectives: 122 us -> none  [the longest x1 19.5 us: on_device(): lax.all_gather(b_up, 'fsdp', axis=0, tiled=True)]
    dot_general x100 -> x14, matrix products: 149 us -> 32.3 us  [dims(): lax.dot_general(matrix, other, (((left,), (right,)), ((), ())), preferred...]
    psum x1 -> x0, waiting for transfers between devices: 93.7 us -> none  [on_device(): lax.psum((shares[0], shares[1], shares[2], shares[3], shares[4], shares[5...]
    dynamic_update_slice x0 -> x33, local copies, waits for them, and re-layouts: none -> 47.8 us  [the longest x32 47.7 us: place(): held = lax.dynamic_update_slice(held, part[None, low:high], (at, 0, 0))]
    all_to_all x0 -> x9, starting transfers between devices: none -> 45.1 us  [the longest x1 9.55 us: on_device(): back = lax.all_to_all(sent, 'ctx', 0, 0, tiled=True)]
  transfers between devices with their start and end apart: 77 -> 60, of which waited for: 48 -> 15; matrix products, arithmetic and copies ran while one was open for 9% -> 28% of each run, Pallas kernels for 0% -> 6%
where the time goes in v1:
time: 574 us; the launch traced here: 564 us
  starting transfers between devices  149 us (26%)
  waiting for transfers between devices  133 us (23%)
  local copies, waits for them, and re-layouts  112 us (20%)
  blocking collectives  66.2 us (12%)
  other arithmetic  37.7 us (7%)
  matrix products  32.3 us (6%)
  Pallas kernels  31.7 us (6%)
    ppermute x33, waiting for transfers between devices, over_fsdp(): return lax.ppermute(block, 'fsdp', route)  92 us
    ppermute x33, starting transfers between devices, over_fsdp(): return lax.ppermute(block, 'fsdp', route)  73.8 us
    psum x1, blocking collectives, on_device(): vector_grads = lax.psum(vector_grads, ('ctx', 'fsdp'))  66.2 us
    dynamic_update_slice x32, local copies, waits for them, and re-layouts, place(): held = lax.dynamic_update_slice(held, part[None, low:high], (at, 0, 0))  47.7 us
    dot_general x14, matrix products, dims(): lax.dot_general(matrix, other, (((left,), (right,)), ((), ())), preferred...  32.3 us
    pallas_call x3, Pallas kernels, call(): pl.pallas_call(kernel, out_shape=[jax.ShapeDtypeStruct(shape, dtype) for...  31.7 us
    ppermute x18, starting transfers between devices, over_ctx(): return lax.ppermute(block, 'ctx', route)  30 us
    all_to_all x1, waiting for transfers between devices, on_device(): lax.all_to_all(jnp.broadcast_to(message[None], (8, 72, WIDTH)), 'ctx', 0,...  14.5 us
  transfers between devices with their start and end apart: 60, of which 15 were waited for; matrix products, arithmetic and copies ran while one was open for 28% of the time, Pallas kernels for 6%

profile of v1, /device:TPU:1, one launch (start us, length us, event | category | flops | bytes accessed | tf_op | source)
XLA Modules:
  0.0 563.6 jit_solution(2178642446560047725)
XLA Ops:
  3.4 2.0 collective-permute-start.20
  7.1 2.1 collective-permute-start.23
  19.7 3.5 all-to-all-start
  23.2 2.5 collective-permute-start
  30.5 2.6 broadcast_in_dim.191
  35.0 2.2 broadcast_in_dim.200
  49.0 3.1 collective-permute-done.22
  54.2 2.6 collective-permute-start.2
  63.9 7.8 %collective-permute-start.4 = (bf16[256,1024]{1,0:T(8,128)(2,1)S(1)}, bf16[256,1024]{1,0:T(8,128)(2,1)S(1)}, u32[]{:S(2)}, u32[]{:S(2)}) collective-permute-start(bf16[256,1024]{1,0:T(8,128)(2,1)S(1)} %pad_maximum_fusion.10.refs_0_), channel_id=1, source_target_pairs={{0,8},{8,0},{16,24},{24,16},{32,40},{40,32},{48,56},{56,48},{64,72... | collective-permute-start | bytes 1572872 | tf_op jit(solution)/shard_map/ppermute | solution.py:29
  71.7 4.5 collective-permute-done.2.refs_2_
  76.2 4.7 collective-permute-start.5
  96.0 13.8 %shard_map.296 = (bf16[192,2048]{1,0:T(8,128)(2,1)}, bf16[2048,128]{1,0:T(8,128)(2,1)S(1)}, bf16[16,64,128]{2,1,0:T(8,128)(2,1)}, f32[64,2048]{1,0:T(8,128)S(1)}, f32[1,2048]{1,0:T(1,128)S(1)}) custom-call(s32[16]{0:T(128)S(1)} %stack.187.order, bf16[256,1024]{1,0:T(8,128)(2,1)S(1)} %pad_maximum_fusion.10.refs_0_, ...), custom_call_target="tpu_custom_call" | custom-call | flops 10000000000 | bytes 10000000 | tf_op jit(solution)/shard_map/pallas_call | solution.py:168
  111.4 6.7 %all-to-all-start.1 = ((bf16[16,64,128]{2,1,0:T(8,128)(2,1)}), bf16[16,64,128]{2,1,0:T(8,128)(2,1)S(1)}, u32[]{:S(2)}, u32[]{:S(2)}) async-start(bf16[16,64,128]{2,1,0:T(8,128)(2,1)} %get-tuple-element.24), calls=%async_computation.1 | async-start | bytes 524288 | tf_op jit(solution)/shard_map/all_to_all | solution.py:301
  123.0 44.8 %collective-permute-done.12 = bf16[576,1024]{1,0:T(8,128)(2,1)} collective-permute-done((bf16[576,1024]{1,0:T(8,128)(2,1)}, bf16[576,1024]{1,0:T(8,128)(2,1)}, u32[]{:S(2)}, u32[]{:S(2)}) %collective-permute-start.12) | collective-permute-done | bytes 1179680 | tf_op jit(solution)/shard_map/ppermute | solution.py:34
  172.5 2.0 collective-permute-start.15
  181.9 1.9 fusion.46
  183.7 1.9 fusion.45
  185.6 1.9 fusion.44
  187.5 1.9 fusion.43
  192.3 2.1 fusion.120
  198.6 2.3 fusion.53
  200.9 2.7 fusion.54
  204.1 3.5 fusion.121
  210.6 35.6 %collective-permute-start.37 = (bf16[128,1024]{1,0:T(8,128)(2,1)S(1)}, bf16[128,1024]{1,0:T(8,128)(2,1)S(1)}, u32[]{:S(2)}, u32[]{:S(2)}) collective-permute-start(bf16[128,1024]{1,0:T(8,128)(2,1)S(1)} %fusion.52), channel_id=1, source_target_pairs={{0,6},{1,7},{2,0},{3,1},{4,2},{5,3},{6,4},{7,5},{8,14},{9,15},{10,... | collective-permute-start | bytes 786440 | tf_op jit(solution)/shard_map/ppermute | solution.py:34
  247.1 2.2 collective-permute-start.30
  251.9 5.8 %collective-permute-done.37 = bf16[128,1024]{1,0:T(8,128)(2,1)S(1)} collective-permute-done((bf16[128,1024]{1,0:T(8,128)(2,1)S(1)}, bf16[128,1024]{1,0:T(8,128)(2,1)S(1)}, u32[]{:S(2)}, u32[]{:S(2)}) %collective-permute-start.37) | collective-permute-done | bytes 262176 | tf_op jit(solution)/shard_map/ppermute | solution.py:34
  258.6 3.4 collective-permute-start.44
  265.3 3.6 collective-permute-done.30
  270.1 2.6 collective-permute-done.28
  273.8 2.3 copy.101
  277.6 4.9 convert_reduce_fusion
  282.4 2.3 fusion.37
  284.8 2.3 convolution_add_fusion
  289.0 2.4 collective-permute-start.41
  293.5 2.4 fusion.104
  295.9 2.3 collective-permute-start.19
  301.1 3.9 copy.93
  307.1 3.1 fusion.12
  310.3 2.3 multiply_reduce_fusion
  314.5 1.9 collective-permute-start.46
  317.4 13.9 %collective-permute-done.42 = bf16[256,128]{1,0:T(8,128)(2,1)S(1)} collective-permute-done((bf16[256,128]{1,0:T(8,128)(2,1)S(1)}, bf16[256,128]{1,0:T(8,128)(2,1)S(1)}, u32[]{:S(2)}, u32[]{:S(2)}) %collective-permute-start.42) | collective-permute-done | bytes 65568 | tf_op jit(solution)/shard_map/ppermute | solution.py:34
  334.7 2.7 collective-permute-done.48
  346.7 4.8 all-to-all-start.2
  352.8 16.8 %collective-permute-done.49 = bf16[8,72,1024]{2,1,0:T(8,128)(2,1)} collective-permute-done((bf16[8,72,1024]{2,1,0:T(8,128)(2,1)}, bf16[8,72,1024]{2,1,0:T(8,128)(2,1)}, u32[]{:S(2)}, u32[]{:S(2)}) %collective-permute-start.49) | collective-permute-done | bytes 1179680 | tf_op jit(solution)/shard_map/ppermute | solution.py:34
  369.6 3.0 fusion.1
  374.4 4.3 all-to-all-start.6
  380.9 14.7 %shard_map.297 = (bf16[16,192,128]{2,1,0:T(8,128)(2,1)}, bf16[192,2048]{1,0:T(8,128)(2,1)S(1)}) custom-call(s32[16]{0:T(128)S(1)} %stack.187.order, bf16[16,64,128]{2,1,0:T(8,128)(2,1)S(1)} %all-to-all-done.2.grad_ref, bf16[192,2048]{1,0:T(8,128)(2,1)S(1)} %copy-done.11, bf16[2048,128]{1,0:T(8,128)(2,1)S(1)} %copy-done.13, f32[64,2048]{1,0:T(8,128)S(1)} %copy-done.15, ...), custom_call_target="tpu_custom_call" | custom-call | flops 10000000000 | bytes 10000000 | tf_op jit(solution)/shard_map/pallas_call | solution.py:168
  396.4 3.2 shard_map.298
  399.6 3.5 all-to-all-start.4
  405.3 6.0 %all-to-all-done.4 = bf16[8,208,128]{2,1,0:T(8,128)(2,1)S(1)} async-done(((bf16[8,208,128]{2,1,0:T(8,128)(2,1)}), bf16[8,208,128]{2,1,0:T(8,128)(2,1)S(1)}, u32[]{:S(2)}, u32[]{:S(2)}) %all-to-all-start.4) | async-done | bytes 426016 | tf_op jit(solution)/shard_map/all_to_all | solution.py:353
  411.2 3.3 all-to-all-start.7
  414.5 4.9 select_bitcast_fusion
  419.5 9.5 %all-to-all-start.3 = ((bf16[16,192,128]{2,1,0:T(8,128)(2,1)}), bf16[16,192,128]{2,1,0:T(8,128)(2,1)}, u32[]{:S(2)}, u32[]{:S(2)}) async-start(bf16[16,192,128]{2,1,0:T(8,128)(2,1)} %get-tuple-element.29), calls=%async_computation.3 | async-start | bytes 1572864 | tf_op jit(solution)/shard_map/all_to_all | solution.py:343
  429.0 2.1 pad_maximum_fusion
  434.6 66.2 %psum.7 = f32[8,10,128]{2,1,0:T(8,128)S(1)} all-reduce(f32[8,10,128]{2,1,0:T(8,128)S(1)} %pad_maximum_fusion.19), channel_id=1, replica_groups=mesh['ctx'=16,'fsdp'=8] {'ctx','fsdp'}, use_global_device_ids=true, to_apply=%region_17.18 | all-reduce | flops 10240 | bytes 81920 | tf_op jit(solution)/shard_map/psum | solution.py:454
  502.1 4.2 all-to-all-start.8
  507.7 1.9 fusion.113
  509.5 14.5 %all-to-all-done.8 = bf16[8,72,1024]{2,1,0:T(8,128)(2,1)} async-done(((bf16[8,72,1024]{2,1,0:T(8,128)(2,1)}), bf16[8,72,1024]{2,1,0:T(8,128)(2,1)}, u32[]{:S(2)}, u32[]{:S(2)}) %all-to-all-start.8) | async-done | bytes 1179680 | tf_op jit(solution)/shard_map/all_to_all | solution.py:423
  525.1 5.3 all-to-all-start.5
  530.4 2.6 convolution_multiply_fusion.1
  536.1 9.5 %all-to-all-done.5 = bf16[16,208,128]{2,1,0:T(8,128)(2,1)S(1)} async-done(((bf16[16,208,128]{2,1,0:T(8,128)(2,1)}), bf16[16,208,128]{2,1,0:T(8,128)(2,1)S(1)}, u32[]{:S(2)}, u32[]{:S(2)}) %all-to-all-start.5) | async-done | bytes 852000 | tf_op jit(solution)/shard_map/all_to_all | solution.py:356
  554.5 2.8 reshape.290
  557.3 3.2 copy.108
  560.5 2.7 reshape.291
  (320 shorter events, 149.5 us)
Async XLA Ops:
  0.7 25.0 %copy-start.31 = (bf16[128,4096]{1,0:T(8,128)(2,1)S(1)}, bf16[128,4096]{1,0:T(8,128)(2,1)}, u32[]{:S(2)}) copy-start(bf16[128,4096]{1,0:T(8,128)(2,1)} %param.27) | copy-start | bytes 3145732
  3.4 39.2 %collective-permute-start.20 = (bf16[192,1024]{1,0:T(8,128)(2,1)}, bf16[192,1024]{1,0:T(8,128)(2,1)}, u32[]{:S(2)}, u32[]{:S(2)}) collective-permute-start(bf16[192,1024]{1,0:T(8,128)(2,1)} %pad_maximum_fusion.13), channel_id=1, source_target_pairs={{0,1},{1,0},{2,3},{3,2},{4,5},{5,4},{6,7},{7,6},{8,9},{9,8},{10,11... | collective-permute-start | bytes 1179656 | tf_op jit(solution)/shard_map/ppermute | solution.py:34
  5.4 40.3 %collective-permute-start.21 = (bf16[192,1024]{1,0:T(8,128)(2,1)}, bf16[192,1024]{1,0:T(8,128)(2,1)}, u32[]{:S(2)}, u32[]{:S(2)}) collective-permute-start(bf16[192,1024]{1,0:T(8,128)(2,1)} %pad_maximum_fusion.13), channel_id=1, source_target_pairs={{0,2},{1,3},{2,4},{3,5},{4,6},{5,7},{6,0},{7,1},{8,10},{9,11},{10,... | collective-permute-start | bytes 1179656 | tf_op jit(solution)/shard_map/ppermute | solution.py:34
  7.1 45.9 %collective-permute-start.23 = (bf16[192,1024]{1,0:T(8,128)(2,1)}, bf16[192,1024]{1,0:T(8,128)(2,1)}, u32[]{:S(2)}, u32[]{:S(2)}) collective-permute-start(bf16[192,1024]{1,0:T(8,128)(2,1)} %pad_maximum_fusion.13), channel_id=1, source_target_pairs={{0,6},{1,7},{2,0},{3,1},{4,2},{5,3},{6,4},{7,5},{8,14},{9,15},{10,... | collective-permute-start | bytes 1179656 | tf_op jit(solution)/shard_map/ppermute | solution.py:34
  9.2 45.0 %collective-permute-start.25 = (bf16[192,1024]{1,0:T(8,128)(2,1)}, bf16[192,1024]{1,0:T(8,128)(2,1)}, u32[]{:S(2)}, u32[]{:S(2)}) collective-permute-start(bf16[192,1024]{1,0:T(8,128)(2,1)} %pad_maximum_fusion.13), channel_id=1, source_target_pairs={{0,4},{1,5},{2,6},{3,7},{4,0},{5,1},{6,2},{7,3},{8,12},{9,13},{10,... | collective-permute-start | bytes 1179656 | tf_op jit(solution)/shard_map/ppermute | solution.py:34
  19.7 22.5 %all-to-all-start = ((bf16[8,208,128]{2,1,0:T(8,128)(2,1)}), bf16[8,208,128]{2,1,0:T(8,128)(2,1)S(1)}, u32[]{:S(2)}, u32[]{:S(2)}) async-start(bf16[8,208,128]{2,1,0:T(8,128)(2,1)} %broadcast_in_dim.165), calls=%async_computation | async-start | bytes 851968 | tf_op jit(solution)/shard_map/all_to_all | solution.py:226
  23.2 17.2 %collective-permute-start = (bf16[128,1024]{1,0:T(8,128)(2,1)}, bf16[128,1024]{1,0:T(8,128)(2,1)}, u32[]{:S(2)}, u32[]{:S(2)}) collective-permute-start(bf16[128,1024]{1,0:T(8,128)(2,1)} %bitcast), channel_id=1, source_target_pairs={{0,16},{8,24},{16,0},{24,8},{32,48},{40,56},{48,32},{56,40},{64,80... | collective-permute-start | bytes 786440 | tf_op jit(solution)/shard_map/ppermute | solution.py:29
  40.4 40.6 %collective-permute-start.8 = (bf16[576,1024]{1,0:T(8,128)(2,1)}, bf16[576,1024]{1,0:T(8,128)(2,1)}, u32[]{:S(2)}, u32[]{:S(2)}) collective-permute-start(bf16[576,1024]{1,0:T(8,128)(2,1)} %pad_maximum_fusion.4), channel_id=1, source_target_pairs={{0,1},{1,0},{2,3},{3,2},{4,5},{5,4},{6,7},{7,6},{8,9},{9,8},{10,11... | collective-permute-start | bytes 3538952 | tf_op jit(solution)/shard_map/ppermute | solution.py:34
  42.6 9.5 %collective-permute-start.22 = (bf16[192,1024]{1,0:T(8,128)(2,1)}, bf16[192,1024]{1,0:T(8,128)(2,1)S(1)}, u32[]{:S(2)}, u32[]{:S(2)}) collective-permute-start(bf16[192,1024]{1,0:T(8,128)(2,1)} %collective-permute-done.20), channel_id=1, source_target_pairs={{0,2},{1,3},{2,4},{3,5},{4,6},{5,7},{6,0},{7,1},{8,10},{9,11},{10,... | collective-permute-start | bytes 1179656 | tf_op jit(solution)/shard_map/ppermute | solution.py:34
  45.7 11.1 %collective-permute-start.24 = (bf16[192,1024]{1,0:T(8,128)(2,1)}, bf16[192,1024]{1,0:T(8,128)(2,1)S(1)}, u32[]{:S(2)}, u32[]{:S(2)}) collective-permute-start(bf16[192,1024]{1,0:T(8,128)(2,1)} %collective-permute-done.20), channel_id=1, source_target_pairs={{0,6},{1,7},{2,0},{3,1},{4,2},{5,3},{6,4},{7,5},{8,14},{9,15},{10,... | collective-permute-start | bytes 1179656 | tf_op jit(solution)/shard_map/ppermute | solution.py:34
  52.1 31.3 %collective-permute-start.9 = (bf16[576,1024]{1,0:T(8,128)(2,1)}, bf16[576,1024]{1,0:T(8,128)(2,1)S(1)}, u32[]{:S(2)}, u32[]{:S(2)}) collective-permute-start(bf16[576,1024]{1,0:T(8,128)(2,1)} %pad_maximum_fusion.4), channel_id=1, source_target_pairs={{0,2},{1,3},{2,4},{3,5},{4,6},{5,7},{6,0},{7,1},{8,10},{9,11},{10,... | collective-permute-start | bytes 3538952 | tf_op jit(solution)/shard_map/ppermute | solution.py:34
  52.9 10.9 %collective-permute-start.1 = (bf16[256,1024]{1,0:T(8,128)(2,1)S(1)}, bf16[256,1024]{1,0:T(8,128)(2,1)S(1)}, u32[]{:S(2)}, u32[]{:S(2)}) collective-permute-start(bf16[256,1024]{1,0:T(8,128)(2,1)S(1)} %pad_maximum_fusion.10.refs_0_), channel_id=1, source_target_pairs={{0,32},{8,40},{16,48},{24,56},{32,64},{40,72},{48,80},{56,88},{64,... | collective-permute-start | bytes 1572872 | tf_op jit(solution)/shard_map/ppermute | solution.py:29
  54.2 22.0 %collective-permute-start.2 = (bf16[256,1024]{1,0:T(8,128)(2,1)S(1)}, bf16[256,1024]{1,0:T(8,128)(2,1)S(1)}, u32[]{:S(2)}, u32[]{:S(2)}) collective-permute-start(bf16[256,1024]{1,0:T(8,128)(2,1)S(1)} %pad_maximum_fusion.10.refs_0_), channel_id=1, source_target_pairs={{0,64},{8,72},{16,80},{24,88},{32,96},{40,104},{48,112},{56,120},{... | collective-permute-start | bytes 1572872 | tf_op jit(solution)/shard_map/ppermute | solution.py:29
  56.9 24.1 %collective-permute-start.3 = (bf16[256,1024]{1,0:T(8,128)(2,1)S(1)}, bf16[256,1024]{1,0:T(8,128)(2,1)S(1)}, u32[]{:S(2)}, u32[]{:S(2)}) collective-permute-start(bf16[256,1024]{1,0:T(8,128)(2,1)S(1)} %pad_maximum_fusion.10.refs_0_), channel_id=1, source_target_pairs={{0,96},{8,104},{16,112},{24,120},{32,0},{40,8},{48,16},{56,24},{64... | collective-permute-start | bytes 1572872 | tf_op jit(solution)/shard_map/ppermute | solution.py:29
  63.9 25.8 %collective-permute-start.4 = (bf16[256,1024]{1,0:T(8,128)(2,1)S(1)}, bf16[256,1024]{1,0:T(8,128)(2,1)S(1)}, u32[]{:S(2)}, u32[]{:S(2)}) collective-permute-start(bf16[256,1024]{1,0:T(8,128)(2,1)S(1)} %pad_maximum_fusion.10.refs_0_), channel_id=1, source_target_pairs={{0,8},{8,0},{16,24},{24,16},{32,40},{40,32},{48,56},{56,48},{64,72... | collective-permute-start | bytes 1572872 | tf_op jit(solution)/shard_map/ppermute | solution.py:29
  76.2 15.6 %collective-permute-start.5 = (bf16[256,1024]{1,0:T(8,128)(2,1)S(1)}, bf16[256,1024]{1,0:T(8,128)(2,1)S(1)}, u32[]{:S(2)}, u32[]{:S(2)}) collective-permute-start(bf16[256,1024]{1,0:T(8,128)(2,1)S(1)} %collective-permute-done.1.refs_1_), channel_id=1, source_target_pairs={{0,8},{8,0},{16,24},{24,16},{32,40},{40,32},{48,56},{56,48},{64,72... | collective-permute-start | bytes 1572872 | tf_op jit(solution)/shard_map/ppermute | solution.py:29
  81.0 12.1 %collective-permute-start.6 = (bf16[256,1024]{1,0:T(8,128)(2,1)S(1)}, bf16[256,1024]{1,0:T(8,128)(2,1)S(1)}, u32[]{:S(2)}, u32[]{:S(2)}) collective-permute-start(bf16[256,1024]{1,0:T(8,128)(2,1)S(1)} %collective-permute-done.2.refs_2_), channel_id=1, source_target_pairs={{0,8},{8,0},{16,24},{24,16},{32,40},{40,32},{48,56},{56,48},{64,72... | collective-permute-start | bytes 1572872 | tf_op jit(solution)/shard_map/ppermute | solution.py:29
  81.0 13.2 %collective-permute-start.7 = (bf16[256,1024]{1,0:T(8,128)(2,1)S(1)}, bf16[256,1024]{1,0:T(8,128)(2,1)S(1)}, u32[]{:S(2)}, u32[]{:S(2)}) collective-permute-start(bf16[256,1024]{1,0:T(8,128)(2,1)S(1)} %collective-permute-done.3.refs_3_), channel_id=1, source_target_pairs={{0,8},{8,0},{16,24},{24,16},{32,40},{40,32},{48,56},{56,48},{64,72... | collective-permute-start | bytes 1572872 | tf_op jit(solution)/shard_map/ppermute | solution.py:29
  83.3 34.8 %collective-permute-start.10 = (bf16[576,1024]{1,0:T(8,128)(2,1)}, bf16[576,1024]{1,0:T(8,128)(2,1)}, u32[]{:S(2)}, u32[]{:S(2)}) collective-permute-start(bf16[576,1024]{1,0:T(8,128)(2,1)} %collective-permute-done.8), channel_id=1, source_target_pairs={{0,2},{1,3},{2,4},{3,5},{4,6},{5,7},{6,0},{7,1},{8,10},{9,11},{10,... | collective-permute-start | bytes 3538952 | tf_op jit(solution)/shard_map/ppermute | solution.py:34
  89.7 31.8 %collective-permute-start.11 = (bf16[576,1024]{1,0:T(8,128)(2,1)}, bf16[576,1024]{1,0:T(8,128)(2,1)}, u32[]{:S(2)}, u32[]{:S(2)}) collective-permute-start(bf16[576,1024]{1,0:T(8,128)(2,1)} %pad_maximum_fusion.4), channel_id=1, source_target_pairs={{0,6},{1,7},{2,0},{3,1},{4,2},{5,3},{6,4},{7,5},{8,14},{9,15},{10,... | collective-permute-start | bytes 3538952 | tf_op jit(solution)/shard_map/ppermute | solution.py:34
  91.8 77.6 %collective-permute-start.13 = (bf16[576,1024]{1,0:T(8,128)(2,1)}, bf16[576,1024]{1,0:T(8,128)(2,1)}, u32[]{:S(2)}, u32[]{:S(2)}) collective-permute-start(bf16[576,1024]{1,0:T(8,128)(2,1)} %pad_maximum_fusion.4), channel_id=1, source_target_pairs={{0,4},{1,5},{2,6},{3,7},{4,0},{5,1},{6,2},{7,3},{8,12},{9,13},{10,... | collective-permute-start | bytes 3538952 | tf_op jit(solution)/shard_map/ppermute | solution.py:34
  93.1 74.7 %collective-permute-start.12 = (bf16[576,1024]{1,0:T(8,128)(2,1)}, bf16[576,1024]{1,0:T(8,128)(2,1)}, u32[]{:S(2)}, u32[]{:S(2)}) collective-permute-start(bf16[576,1024]{1,0:T(8,128)(2,1)} %collective-permute-done.8), channel_id=1, source_target_pairs={{0,6},{1,7},{2,0},{3,1},{4,2},{5,3},{6,4},{7,5},{8,14},{9,15},{10,... | collective-permute-start | bytes 3538952 | tf_op jit(solution)/shard_map/ppermute | solution.py:34
  94.2 76.7 %collective-permute-start.14 = (bf16[576,1024]{1,0:T(8,128)(2,1)}, bf16[576,1024]{1,0:T(8,128)(2,1)}, u32[]{:S(2)}, u32[]{:S(2)}) collective-permute-start(bf16[576,1024]{1,0:T(8,128)(2,1)} %collective-permute-done.8), channel_id=1, source_target_pairs={{0,4},{1,5},{2,6},{3,7},{4,0},{5,1},{6,2},{7,3},{8,12},{9,13},{10,... | collective-permute-start | bytes 3538952 | tf_op jit(solution)/shard_map/ppermute | solution.py:34
  111.4 80.8 %all-to-all-start.1 = ((bf16[16,64,128]{2,1,0:T(8,128)(2,1)}), bf16[16,64,128]{2,1,0:T(8,128)(2,1)S(1)}, u32[]{:S(2)}, u32[]{:S(2)}) async-start(bf16[16,64,128]{2,1,0:T(8,128)(2,1)} %get-tuple-element.24), calls=%async_computation.1 | async-start | bytes 524288 | tf_op jit(solution)/shard_map/all_to_all | solution.py:301
  118.1 90.1 %collective-permute-start.26 = (bf16[192,1024]{1,0:T(8,128)(2,1)}, bf16[192,1024]{1,0:T(8,128)(2,1)}, u32[]{:S(2)}, u32[]{:S(2)}) collective-permute-start(bf16[192,1024]{1,0:T(8,128)(2,1)} %collective-permute-done.20), channel_id=1, source_target_pairs={{0,4},{1,5},{2,6},{3,7},{4,0},{5,1},{6,2},{7,3},{8,12},{9,13},{10,... | collective-permute-start | bytes 1179656 | tf_op jit(solution)/shard_map/ppermute | solution.py:34
  172.5 16.9 %collective-permute-start.15 = (bf16[8,64,1024]{2,1,0:T(8,128)(2,1)}, bf16[8,64,1024]{2,1,0:T(8,128)(2,1)S(1)}, u32[]{:S(2)}, u32[]{:S(2)}) collective-permute-start(bf16[8,64,1024]{2,1,0:T(8,128)(2,1)} %fusion.79), channel_id=1, source_target_pairs={{0,8},{8,0},{16,24},{24,16},{32,40},{40,32},{48,56},{56,48},{64,72... | collective-permute-start | bytes 3145736 | tf_op jit(solution)/shard_map/ppermute | solution.py:29
  194.8 3.8 collective-permute-start.16
  207.6 41.7 %collective-permute-start.17 = (f32[128,1024]{1,0:T(8,128)S(1)}, f32[128,1024]{1,0:T(8,128)S(1)}, u32[]{:S(2)}, u32[]{:S(2)}) collective-permute-start(f32[128,1024]{1,0:T(8,128)S(1)} %slice.380), channel_id=1, source_target_pairs={{0,8},{8,0},{16,24},{24,16},{32,40},{40,32},{48,56},{56,48},{64,72... | collective-permute-start | bytes 1572872 | tf_op jit(solution)/shard_map/ppermute | solution.py:29
  210.6 47.0 %collective-permute-start.37 = (bf16[128,1024]{1,0:T(8,128)(2,1)S(1)}, bf16[128,1024]{1,0:T(8,128)(2,1)S(1)}, u32[]{:S(2)}, u32[]{:S(2)}) collective-permute-start(bf16[128,1024]{1,0:T(8,128)(2,1)S(1)} %fusion.52), channel_id=1, source_target_pairs={{0,6},{1,7},{2,0},{3,1},{4,2},{5,3},{6,4},{7,5},{8,14},{9,15},{10,... | collective-permute-start | bytes 786440 | tf_op jit(solution)/shard_map/ppermute | solution.py:34
  246.3 12.4 %collective-permute-start.36 = (bf16[128,1024]{1,0:T(8,128)(2,1)S(1)}, bf16[128,1024]{1,0:T(8,128)(2,1)S(1)}, u32[]{:S(2)}, u32[]{:S(2)}) collective-permute-start(bf16[128,1024]{1,0:T(8,128)(2,1)S(1)} %fusion.52), channel_id=1, source_target_pairs={{0,4},{1,5},{2,6},{3,7},{4,0},{5,1},{6,2},{7,3},{8,12},{9,13},{10,... | collective-permute-start | bytes 786440 | tf_op jit(solution)/shard_map/ppermute | solution.py:34
  246.3 15.8 %collective-permute-start.35 = (bf16[128,1024]{1,0:T(8,128)(2,1)S(1)}, bf16[128,1024]{1,0:T(8,128)(2,1)S(1)}, u32[]{:S(2)}, u32[]{:S(2)}) collective-permute-start(bf16[128,1024]{1,0:T(8,128)(2,1)S(1)} %fusion.52), channel_id=1, source_target_pairs={{0,2},{1,3},{2,4},{3,5},{4,6},{5,7},{6,0},{7,1},{8,10},{9,11},{10,... | collective-permute-start | bytes 786440 | tf_op jit(solution)/shard_map/ppermute | solution.py:34
  247.1 21.8 %collective-permute-start.30 = (bf16[256,512]{1,0:T(8,128)(2,1)S(1)}, bf16[256,512]{1,0:T(8,128)(2,1)S(1)}, u32[]{:S(2)}, u32[]{:S(2)}) collective-permute-start(bf16[256,512]{1,0:T(8,128)(2,1)S(1)} %get-tuple-element.116), channel_id=1, source_target_pairs={{0,6},{1,7},{2,0},{3,1},{4,2},{5,3},{6,4},{7,5},{8,14},{9,15},{10,... | collective-permute-start | bytes 786440 | tf_op jit(solution)/shard_map/ppermute | solution.py:34
  249.3 20.8 %collective-permute-start.29 = (bf16[256,512]{1,0:T(8,128)(2,1)S(1)}, bf16[256,512]{1,0:T(8,128)(2,1)S(1)}, u32[]{:S(2)}, u32[]{:S(2)}) collective-permute-start(bf16[256,512]{1,0:T(8,128)(2,1)S(1)} %get-tuple-element.117), channel_id=1, source_target_pairs={{0,4},{1,5},{2,6},{3,7},{4,0},{5,1},{6,2},{7,3},{8,12},{9,13},{10,... | collective-permute-start | bytes 786440 | tf_op jit(solution)/shard_map/ppermute | solution.py:34
  257.7 15.1 %collective-permute-start.28 = (bf16[256,512]{1,0:T(8,128)(2,1)S(1)}, bf16[256,512]{1,0:T(8,128)(2,1)S(1)}, u32[]{:S(2)}, u32[]{:S(2)}) collective-permute-start(bf16[256,512]{1,0:T(8,128)(2,1)S(1)} %get-tuple-element.118), channel_id=1, source_target_pairs={{0,2},{1,3},{2,4},{3,5},{4,6},{5,7},{6,0},{7,1},{8,10},{9,11},{10,... | collective-permute-start | bytes 786440 | tf_op jit(solution)/shard_map/ppermute | solution.py:34
  258.6 57.8 %collective-permute-start.44 = (bf16[256,128]{1,0:T(8,128)(2,1)}, bf16[256,128]{1,0:T(8,128)(2,1)}, u32[]{:S(2)}, u32[]{:S(2)}) collective-permute-start(bf16[256,128]{1,0:T(8,128)(2,1)} %get-tuple-element.140), channel_id=1, source_target_pairs={{0,6},{1,7},{2,0},{3,1},{4,2},{5,3},{6,4},{7,5},{8,14},{9,15},{10,... | collective-permute-start | bytes 196616 | tf_op jit(solution)/shard_map/ppermute | solution.py:34
  262.0 14.9 %collective-permute-start.18 = (bf16[128,1024]{1,0:T(8,128)(2,1)}, bf16[128,1024]{1,0:T(8,128)(2,1)}, u32[]{:S(2)}, u32[]{:S(2)}) collective-permute-start(bf16[128,1024]{1,0:T(8,128)(2,1)} %get-tuple-element.75), channel_id=1, source_target_pairs={{0,8},{8,0},{16,24},{24,16},{32,40},{40,32},{48,56},{56,48},{64,72... | collective-permute-start | bytes 786440 | tf_op jit(solution)/shard_map/ppermute | solution.py:29
  268.9 27.0 %collective-permute-start.38 = (bf16[4,128,1024]{2,1,0:T(8,128)(2,1)}, bf16[4,128,1024]{2,1,0:T(8,128)(2,1)}, u32[]{:S(2)}, u32[]{:S(2)}) collective-permute-start(bf16[4,128,1024]{2,1,0:T(8,128)(2,1)} %get-tuple-element.126), channel_id=1, source_target_pairs={{0,8},{8,0},{16,24},{24,16},{32,40},{40,32},{48,56},{56,48},{64,72... | collective-permute-start | bytes 3145736 | tf_op jit(solution)/shard_map/ppermute | solution.py:29
  276.1 12.9 %collective-permute-start.33 = (bf16[128,1024]{1,0:T(8,128)(2,1)}, bf16[128,1024]{1,0:T(8,128)(2,1)S(1)}, u32[]{:S(2)}, u32[]{:S(2)}) collective-permute-start(bf16[128,1024]{1,0:T(8,128)(2,1)} %get-tuple-element.75), channel_id=1, source_target_pairs={{0,6},{1,7},{2,0},{3,1},{4,2},{5,3},{6,4},{7,5},{8,14},{9,15},{10,... | collective-permute-start | bytes 786440 | tf_op jit(solution)/shard_map/ppermute | solution.py:34
  276.9 14.6 %collective-permute-start.32 = (bf16[128,1024]{1,0:T(8,128)(2,1)}, bf16[128,1024]{1,0:T(8,128)(2,1)S(1)}, u32[]{:S(2)}, u32[]{:S(2)}) collective-permute-start(bf16[128,1024]{1,0:T(8,128)(2,1)} %get-tuple-element.75), channel_id=1, source_target_pairs={{0,4},{1,5},{2,6},{3,7},{4,0},{5,1},{6,2},{7,3},{8,12},{9,13},{10,... | collective-permute-start | bytes 786440 | tf_op jit(solution)/shard_map/ppermute | solution.py:34
  276.9 15.9 %collective-permute-start.31 = (bf16[128,1024]{1,0:T(8,128)(2,1)}, bf16[128,1024]{1,0:T(8,128)(2,1)S(1)}, u32[]{:S(2)}, u32[]{:S(2)}) collective-permute-start(bf16[128,1024]{1,0:T(8,128)(2,1)} %get-tuple-element.75), channel_id=1, source_target_pairs={{0,2},{1,3},{2,4},{3,5},{4,6},{5,7},{6,0},{7,1},{8,10},{9,11},{10,... | collective-permute-start | bytes 786440 | tf_op jit(solution)/shard_map/ppermute | solution.py:34
  289.0 16.0 %collective-permute-start.41 = (bf16[256,512]{1,0:T(8,128)(2,1)}, bf16[256,512]{1,0:T(8,128)(2,1)}, u32[]{:S(2)}, u32[]{:S(2)}) collective-permute-start(bf16[256,512]{1,0:T(8,128)(2,1)} %get-tuple-element.122), channel_id=1, source_target_pairs={{0,6},{1,7},{2,0},{3,1},{4,2},{5,3},{6,4},{7,5},{8,14},{9,15},{10,... | collective-permute-start | bytes 786440 | tf_op jit(solution)/shard_map/ppermute | solution.py:34
  291.4 14.2 %collective-permute-start.40 = (bf16[256,512]{1,0:T(8,128)(2,1)}, bf16[256,512]{1,0:T(8,128)(2,1)}, u32[]{:S(2)}, u32[]{:S(2)}) collective-permute-start(bf16[256,512]{1,0:T(8,128)(2,1)} %get-tuple-element.123), channel_id=1, source_target_pairs={{0,4},{1,5},{2,6},{3,7},{4,0},{5,1},{6,2},{7,3},{8,12},{9,13},{10,... | collective-permute-start | bytes 786440 | tf_op jit(solution)/shard_map/ppermute | solution.py:34
  292.8 14.3 %collective-permute-start.39 = (bf16[256,512]{1,0:T(8,128)(2,1)}, bf16[256,512]{1,0:T(8,128)(2,1)}, u32[]{:S(2)}, u32[]{:S(2)}) collective-permute-start(bf16[256,512]{1,0:T(8,128)(2,1)} %get-tuple-element.124), channel_id=1, source_target_pairs={{0,2},{1,3},{2,4},{3,5},{4,6},{5,7},{6,0},{7,1},{8,10},{9,11},{10,... | collective-permute-start | bytes 786440 | tf_op jit(solution)/shard_map/ppermute | solution.py:34
  295.9 14.3 %collective-permute-start.19 = (f32[128,1024]{1,0:T(8,128)}, f32[128,1024]{1,0:T(8,128)}, u32[]{:S(2)}, u32[]{:S(2)}) collective-permute-start(f32[128,1024]{1,0:T(8,128)} %slice.387), channel_id=1, source_target_pairs={{0,8},{8,0},{16,24},{24,16},{32,40},{40,32},{48,56},{56,48},{64,72... | collective-permute-start | bytes 1572872 | tf_op jit(solution)/shard_map/ppermute | solution.py:29
  305.0 11.5 %collective-permute-start.43 = (bf16[256,128]{1,0:T(8,128)(2,1)}, bf16[256,128]{1,0:T(8,128)(2,1)S(1)}, u32[]{:S(2)}, u32[]{:S(2)}) collective-permute-start(bf16[256,128]{1,0:T(8,128)(2,1)} %get-tuple-element.141), channel_id=1, source_target_pairs={{0,4},{1,5},{2,6},{3,7},{4,0},{5,1},{6,2},{7,3},{8,12},{9,13},{10,... | collective-permute-start | bytes 196616 | tf_op jit(solution)/shard_map/ppermute | solution.py:34
  305.6 28.0 %collective-permute-start.34 = (bf16[4,128,1024]{2,1,0:T(8,128)(2,1)}, bf16[4,128,1024]{2,1,0:T(8,128)(2,1)S(1)}, u32[]{:S(2)}, u32[]{:S(2)}) collective-permute-start(bf16[4,128,1024]{2,1,0:T(8,128)(2,1)} %get-tuple-element.114), channel_id=1, source_target_pairs={{0,8},{8,0},{16,24},{24,16},{32,40},{40,32},{48,56},{56,48},{64,72... | collective-permute-start | bytes 3145736 | tf_op jit(solution)/shard_map/ppermute | solution.py:29
  313.6 18.2 %collective-permute-start.47 = (bf16[128,1024]{1,0:T(8,128)(2,1)S(1)}, bf16[128,1024]{1,0:T(8,128)(2,1)S(1)}, u32[]{:S(2)}, u32[]{:S(2)}) collective-permute-start(bf16[128,1024]{1,0:T(8,128)(2,1)S(1)} %get-tuple-element.77), channel_id=1, source_target_pairs={{0,6},{1,7},{2,0},{3,1},{4,2},{5,3},{6,4},{7,5},{8,14},{9,15},{10,... | collective-permute-start | bytes 786440 | tf_op jit(solution)/shard_map/ppermute | solution.py:34
  314.5 17.3 %collective-permute-start.46 = (bf16[128,1024]{1,0:T(8,128)(2,1)S(1)}, bf16[128,1024]{1,0:T(8,128)(2,1)S(1)}, u32[]{:S(2)}, u32[]{:S(2)}) collective-permute-start(bf16[128,1024]{1,0:T(8,128)(2,1)S(1)} %get-tuple-element.77), channel_id=1, source_target_pairs={{0,4},{1,5},{2,6},{3,7},{4,0},{5,1},{6,2},{7,3},{8,12},{9,13},{10,... | collective-permute-start | bytes 786440 | tf_op jit(solution)/shard_map/ppermute | solution.py:34
  316.4 15.4 %collective-permute-start.45 = (bf16[128,1024]{1,0:T(8,128)(2,1)S(1)}, bf16[128,1024]{1,0:T(8,128)(2,1)S(1)}, u32[]{:S(2)}, u32[]{:S(2)}) collective-permute-start(bf16[128,1024]{1,0:T(8,128)(2,1)S(1)} %get-tuple-element.77), channel_id=1, source_target_pairs={{0,2},{1,3},{2,4},{3,5},{4,6},{5,7},{6,0},{7,1},{8,10},{9,11},{10,... | collective-permute-start | bytes 786440 | tf_op jit(solution)/shard_map/ppermute | solution.py:34
  316.5 14.8 %collective-permute-start.42 = (bf16[256,128]{1,0:T(8,128)(2,1)S(1)}, bf16[256,128]{1,0:T(8,128)(2,1)S(1)}, u32[]{:S(2)}, u32[]{:S(2)}) collective-permute-start(bf16[256,128]{1,0:T(8,128)(2,1)S(1)} %copy-done.37), channel_id=1, source_target_pairs={{0,2},{1,3},{2,4},{3,5},{4,6},{5,7},{6,0},{7,1},{8,10},{9,11},{10,... | collective-permute-start | bytes 196616 | tf_op jit(solution)/shard_map/ppermute | solution.py:34
  331.3 83.3 %collective-permute-start.27 = (bf16[8,3,64,1024]{3,2,1,0:T(8,128)(2,1)}, bf16[8,3,64,1024]{3,2,1,0:T(8,128)(2,1)}, u32[]{:S(2)}, u32[]{:S(2)}) collective-permute-start(bf16[8,3,64,1024]{3,2,1,0:T(8,128)(2,1)} %bitcast.91), channel_id=1, source_target_pairs={{0,8},{8,0},{16,24},{24,16},{32,40},{40,32},{48,56},{56,48},{64,72... | collective-permute-start | bytes 9437192 | tf_op jit(solution)/shard_map/ppermute | solution.py:29
  333.1 4.3 collective-permute-start.48
  342.1 27.5 %collective-permute-start.49 = (bf16[8,72,1024]{2,1,0:T(8,128)(2,1)}, bf16[8,72,1024]{2,1,0:T(8,128)(2,1)}, u32[]{:S(2)}, u32[]{:S(2)}) collective-permute-start(bf16[8,72,1024]{2,1,0:T(8,128)(2,1)} %pad_maximum_fusion.5), channel_id=1, source_target_pairs={{0,1},{1,0},{2,3},{3,2},{4,5},{5,4},{6,7},{7,6},{8,9},{9,8},{10,11... | collective-permute-start | bytes 3538952 | tf_op jit(solution)/shard_map/ppermute | solution.py:34
  346.7 27.7 %all-to-all-start.2 = ((bf16[16,64,128]{2,1,0:T(8,128)(2,1)}), bf16[16,64,128]{2,1,0:T(8,128)(2,1)S(1)}, u32[]{:S(2)}, u32[]{:S(2)}) async-start(bf16[16,64,128]{2,1,0:T(8,128)(2,1)} %bitcast.81), calls=%async_computation.2 | async-start | bytes 524288 | tf_op jit(solution)/shard_map/all_to_all | solution.py:329
  374.4 25.2 %all-to-all-start.6 = ((bf16[8,72,1024]{2,1,0:T(8,128)(2,1)}), bf16[8,72,1024]{2,1,0:T(8,128)(2,1)}, u32[]{:S(2)}, u32[]{:S(2)}) async-start(bf16[8,72,1024]{2,1,0:T(8,128)(2,1)} %fusion.1), calls=%async_computation.6 | async-start | bytes 2359296 | tf_op jit(solution)/shard_map/all_to_all | solution.py:413
  380.9 15.6 %copy-start.4 = (bf16[256,1024]{1,0:T(8,128)(2,1)S(1)}, bf16[256,1024]{1,0:T(8,128)(2,1)}, u32[]{:S(2)}) copy-start(bf16[256,1024]{1,0:T(8,128)(2,1)} %copy-done.3) | copy-start | bytes 1572868
  380.9 15.6 %copy-start.6 = (bf16[256,1024]{1,0:T(8,128)(2,1)S(1)}, bf16[256,1024]{1,0:T(8,128)(2,1)}, u32[]{:S(2)}) copy-start(bf16[256,1024]{1,0:T(8,128)(2,1)} %copy-done.5) | copy-start | bytes 1572868
  380.9 15.6 %copy-start.8 = (bf16[256,1024]{1,0:T(8,128)(2,1)S(1)}, bf16[256,1024]{1,0:T(8,128)(2,1)}, u32[]{:S(2)}) copy-start(bf16[256,1024]{1,0:T(8,128)(2,1)} %copy-done.7) | copy-start | bytes 1572868
  399.6 11.6 %all-to-all-start.4 = ((bf16[8,208,128]{2,1,0:T(8,128)(2,1)}), bf16[8,208,128]{2,1,0:T(8,128)(2,1)S(1)}, u32[]{:S(2)}, u32[]{:S(2)}) async-start(bf16[8,208,128]{2,1,0:T(8,128)(2,1)} %shard_map.298), calls=%async_computation.4 | async-start | bytes 851968 | tf_op jit(solution)/shard_map/all_to_all | solution.py:353
  411.2 8.2 %all-to-all-start.7 = ((bf16[4,16,512]{2,1,0:T(8,128)(2,1)}), bf16[4,16,512]{2,1,0:T(8,128)(2,1)S(1)}, u32[]{:S(2)}, u32[]{:S(2)}) async-start(bf16[4,16,512]{2,1,0:T(8,128)(2,1)} %pad_maximum_fusion.17), calls=%async_computation.7 | async-start | bytes 131072 | tf_op jit(solution)/shard_map/all_to_all | solution.py:420
  419.5 81.4 %all-to-all-start.3 = ((bf16[16,192,128]{2,1,0:T(8,128)(2,1)}), bf16[16,192,128]{2,1,0:T(8,128)(2,1)}, u32[]{:S(2)}, u32[]{:S(2)}) async-start(bf16[16,192,128]{2,1,0:T(8,128)(2,1)} %get-tuple-element.29), calls=%async_computation.3 | async-start | bytes 1572864 | tf_op jit(solution)/shard_map/all_to_all | solution.py:343
  502.1 22.0 %all-to-all-start.8 = ((bf16[8,72,1024]{2,1,0:T(8,128)(2,1)}), bf16[8,72,1024]{2,1,0:T(8,128)(2,1)}, u32[]{:S(2)}, u32[]{:S(2)}) async-start(bf16[8,72,1024]{2,1,0:T(8,128)(2,1)} %broadcast_in_dim.211), calls=%async_computation.8 | async-start | bytes 2359296 | tf_op jit(solution)/shard_map/all_to_all | solution.py:423
  525.1 20.5 %all-to-all-start.5 = ((bf16[16,208,128]{2,1,0:T(8,128)(2,1)}), bf16[16,208,128]{2,1,0:T(8,128)(2,1)S(1)}, u32[]{:S(2)}, u32[]{:S(2)}) async-start(bf16[16,208,128]{2,1,0:T(8,128)(2,1)} %broadcast_in_dim.210), calls=%async_computation.5 | async-start | bytes 1703936 | tf_op jit(solution)/shard_map/all_to_all | solution.py:356
  533.9 16.2 %collective-permute-start.50 = (bf16[8,72,1024]{2,1,0:T(8,128)(2,1)}, bf16[8,72,1024]{2,1,0:T(8,128)(2,1)}, u32[]{:S(2)}, u32[]{:S(2)}) collective-permute-start(bf16[8,72,1024]{2,1,0:T(8,128)(2,1)} %all-to-all-done.8), channel_id=1, source_target_pairs={{0,8},{8,0},{16,24},{24,16},{32,40},{40,32},{48,56},{56,48},{64,72... | collective-permute-start | bytes 3538952 | tf_op jit(solution)/shard_map/ppermute | solution.py:29
  (34 other events, 126.7 us)
